TPU v7x, 1024 devices: a whole 8x8x8 slice. The times are simulated.
1024 devices in a mesh: ctx: 64 (over y, x), head: 16 (over z, core).
Axes of the slice: x: 8, y: 8, z: 8, core: 2. Of those that a mesh axis runs over, the one named last changes fastest.
Arguments:
- inputs: bfloat16 [32768, 4096], P('ctx', 'head'), may hold values from -6 to 6
- write_map: bfloat16 [32768, 128], P('ctx'), may hold values from -2 to 2
- read_map: bfloat16 [32768, 128], P('ctx'), may hold values from -2 to 2
- step_scale: float32 [64, 32768], P('head', 'ctx'), may hold values from 0 to 1, as said below
- log_decay: float32 [64, 32768], P('head', 'ctx'), may hold values from -1 to 0, as said below
- lengths: int32 [4], replicated, may hold values from 1 to 16384, 32768 in all
- out_grad: bfloat16 [32768, 4096], P('ctx', 'head'), may hold values from -1.5 to 1.5
Outputs:
- outputs: bfloat16 [32768, 4096], P('ctx', 'head')
- input_grad: bfloat16 [32768, 4096], P('ctx', 'head')
- write_grad: float32 [32768, 128], P(('ctx', 'head'))
- read_grad: float32 [32768, 128], P(('ctx', 'head'))
- step_grad: float32 [64, 32768], P('head', 'ctx')
- decay_grad: float32 [64, 32768], P('head', 'ctx')
Inputs may be any that keep to these rules, and one draw needn't show every extreme that they name: The lengths add up to 32768; the longest is exactly 16384. `log_decay`: zero or negative. `step_scale`: Positive.
All inputs are finite; a program needn't handle non-finite values.
Results may differ from a plain program's by a relative error of at most 0.0019.
Values sent between devices are 32-bit elements; how exact they have to be, the bound alone decides.
No kernel may reach another device: no remote copies, remote signals or barrier semaphores. Data moves between devices by JAX's collectives and lax.ppermute only.
A program may use at most 64 MiB of HBM per device.

v0:
```python
import jax
import jax.numpy as jnp
from jax import lax
from jax.sharding import PartitionSpec as P


def carried_in(part, axis, combine, identity, reverse):
    count = lax.axis_size(axis)
    place = lax.axis_index(axis)
    ahead = count - 1 - place if reverse else place
    gathered = jax.tree.map(lambda a: lax.all_gather(a, axis), part)
    state = jax.tree.map(lambda a, e: jnp.zeros_like(a) + jnp.asarray(e, a.dtype), part, identity)

    def one(lap, state):
        source = count - 1 - lap if reverse else lap
        return combine(
            state, jax.tree.map(lambda a: lax.dynamic_index_in_dim(a, source, 0, False), gathered)
        )

    return lax.fori_loop(0, ahead, one, state)


def combine(earlier, latter):
    return (earlier[0] * latter[0], latter[0][:, None, None] * earlier[1] + latter[1])


def shards(inputs, write_map, read_map, step_scale, log_decay, lengths, out_grad):
    highest = lax.Precision.HIGHEST
    row_count = inputs.shape[0]
    head_count = step_scale.shape[0]
    head_width = inputs.shape[1] // head_count
    offset = lax.axis_index("ctx") * row_count
    record_ends = jnp.cumsum(lengths)
    record_starts = record_ends - lengths
    positions = offset + jnp.arange(row_count, dtype=jnp.int32)
    record_id = jnp.sum((record_starts[None, :] <= positions[:, None]).astype(jnp.int32), axis=1)
    id_prev = jnp.sum((record_starts <= offset - 1).astype(jnp.int32))
    cumulative = jnp.cumsum(log_decay, axis=1)
    enter = jnp.where(record_id[None, :] == id_prev, jnp.exp(cumulative), 0.0)
    leave = jnp.where(
        record_id[None, :] == record_id[-1], jnp.exp(cumulative[:, -1:] - cumulative), 0.0
    )
    keep_factor = jnp.where(record_id[-1] == id_prev, jnp.exp(cumulative[:, -1]), 0.0)
    heads_x = inputs.reshape(row_count, head_count, head_width).transpose(1, 0, 2)
    heads_g = out_grad.reshape(row_count, head_count, head_width).transpose(1, 0, 2)
    x_float = heads_x.astype(jnp.float32)
    g_float = heads_g.astype(jnp.float32)
    write_f = write_map.astype(jnp.float32)
    read_f = read_map.astype(jnp.float32)
    fresh = jnp.einsum(
        "hsp,sn->hpn", x_float * (leave * step_scale)[:, :, None], write_f, precision=highest
    )
    backward_terms = jnp.einsum(
        "hup,un->hpn", g_float * enter[:, :, None], read_f, precision=highest
    )
    forward_in = (keep_factor, fresh)
    backward_in = (keep_factor, backward_terms)
    identity = (jnp.ones_like(keep_factor), jnp.zeros_like(fresh))
    state_pair = carried_in(forward_in, "ctx", combine, identity, False)
    future_pair = carried_in(backward_in, "ctx", combine, identity, True)
    incoming = state_pair[1]
    future = future_pair[1]
    scores = lax.dot_general(
        read_map, write_map, (((1,), (1,)), ((), ())), preferred_element_type=jnp.float32
    )
    position = jnp.arange(row_count, dtype=jnp.int32)
    inside = (position[None, :] <= position[:, None]) & (record_id[:, None] == record_id[None, :])
    inside_f = inside.astype(jnp.float32)

    def per_head(pieces):
        (
            x_head,
            g_head,
            x_f,
            g_f,
            step_rate,
            cum_log,
            enter_h,
            leave_h,
            state_h,
            future_hidden_state,
            raw_decay,
        ) = pieces
        gap_log = jnp.where(inside, cum_log[:, None] - cum_log[None, :], 0.0)
        decays = jnp.exp(gap_log) * inside_f
        weighted = scores * decays
        carried = jnp.dot(read_f, state_h.T, precision=highest)
        result_y = (
            jnp.dot(weighted * step_rate[None, :], x_f, precision=highest)
            + enter_h[:, None] * carried
        )
        pulled = lax.dot_general(weighted, g_f, (((0,), (0,)), ((), ())), precision=highest)
        pulled = pulled + leave_h[:, None] * jnp.dot(
            write_f, future_hidden_state.T, precision=highest
        )
        along_x = jnp.sum(x_f * pulled, axis=1)
        x_grad = step_rate[:, None] * pulled
        pair_dots = lax.dot_general(
            g_head, x_head, (((1,), (1,)), ((), ())), preferred_element_type=jnp.float32
        )
        paired = decays * pair_dots
        x_future = jnp.dot(x_f, future_hidden_state, precision=highest)
        w_grad = step_rate[:, None] * (
            lax.dot_general(paired, read_f, (((0,), (0,)), ((), ())), precision=highest)
            + leave_h[:, None] * x_future
        )
        scaled_pair_products = paired * step_rate[None, :]
        r_grad = jnp.dot(scaled_pair_products, write_f, precision=highest) + enter_h[
            :, None
        ] * jnp.dot(g_f, state_h, precision=highest)
        joint = scaled_pair_products * scores
        col_sums = jnp.sum(joint, axis=0)
        row_sums = jnp.sum(joint, axis=1)
        term_inner = jnp.cumsum(col_sums) - jnp.cumsum(row_sums) + row_sums
        term_future = leave_h * jnp.dot(
            decays, step_rate * jnp.sum(x_future * write_f, axis=1), precision=highest
        )
        term_past = enter_h * lax.dot_general(
            decays, jnp.sum(g_f * carried, axis=1), (((0,), (0,)), ((), ())), precision=highest
        )
        term_both = enter_h * leave_h * jnp.sum(future_hidden_state * state_h)
        decay_total = term_inner + term_future + term_past + term_both - step_rate * along_x
        return (result_y, x_grad, w_grad, r_grad, step_rate * along_x, raw_decay * decay_total)

    results = lax.map(
        per_head,
        (
            heads_x,
            heads_g,
            x_float,
            g_float,
            step_scale,
            cumulative,
            enter,
            leave,
            incoming,
            future,
            log_decay,
        ),
    )
    head_y, head_xgrad, head_wgrad, head_rgrad, step_grad, decay_grad = results
    outputs = (
        head_y.transpose(1, 0, 2).reshape(row_count, head_count * head_width).astype(jnp.bfloat16)
    )
    input_grad = (
        head_xgrad.transpose(1, 0, 2)
        .reshape(row_count, head_count * head_width)
        .astype(jnp.bfloat16)
    )
    write_grad, read_grad = (
        lax.psum_scatter(jnp.sum(head_wgrad, axis=0), "head", scatter_dimension=0, tiled=True),
        lax.psum_scatter(jnp.sum(head_rgrad, axis=0), "head", scatter_dimension=0, tiled=True),
    )
    return (outputs, input_grad, write_grad, read_grad, step_grad, decay_grad)


def solution(mesh):
    placed = (
        P("ctx", "head"),
        P("ctx", None),
        P("ctx", None),
        P("head", "ctx"),
        P("head", "ctx"),
        P(),
        P("ctx", "head"),
    )
    return jax.shard_map(
        shards,
        mesh=mesh,
        in_specs=placed,
        out_specs=(
            P("ctx", "head"),
            P("ctx", "head"),
            P(("ctx", "head"), None),
            P(("ctx", "head"), None),
            P("head", "ctx"),
            P("head", "ctx"),
        ),
        check_vma=False,
    )
```

profile of v0, /device:TPU:1, one launch (start us, length us, event | category | flops | bytes accessed | tf_op | source)
XLA Modules:
  0.0 533.6 jit_solution(9823976295753100442)
XLA Ops:
  8.1 1.3 fusion.100
  10.0 1.3 broadcast_compare_fusion
  13.3 1.2 reduce-window.34
  15.0 1.1 copy.39
  17.0 2.0 fusion.90
  19.1 1.8 copy.38
  20.9 2.0 fusion.92
  23.0 1.8 convert_element_type.41
  24.8 1.0 copy.40
  26.8 1.3 dynamic-slice
  28.9 118.7 %all-reduce = f32[256]{0:T(256)S(1)} all-reduce(f32[256]{0:T(256)S(1)} %dynamic-update-slice), channel_id=2, replica_groups=mesh['ctx'=64,'head'=16] {'ctx'}, use_global_device_ids=true, to_apply=%add | all-reduce | flops 256 | bytes 2048
  147.8 2.3 fusion.103
  150.0 65.7 %while.52 = (s32[]{:T(128)}, f32[4,64,128]{2,1,0:T(8,128)S(1)}, s32[]{:T(128)}, f32[64,4]{1,0:T(8,128)S(1)}, f32[64,4,64,128]{3,2,1,0:T(8,128)}) while((s32[]{:T(128)}, f32[4,64,128]{2,1,0:T(8,128)S(1)}, s32[]{:T(128)}, f32[64,4]{1,0:T(8,128)S(1)}, f32[64,4,64,128]{3,2,1,0:T(8,128)}) %tuple.137), condition=%wide.region_8.9_spmd.clone, body=%wide.region_7.8_spmd.sunk.clone | while | flops 65542 | bytes 393379 | solution.py:20
  158.4 1.0 bitcast_add_fusion.8
  169.9 1.0 bitcast_add_fusion.8
  206.3 1.0 bitcast_add_fusion.8
  209.5 1.0 bitcast_add_fusion.8
  210.5 1.0 bitcast_add_fusion.8
  213.7 1.0 bitcast_add_fusion.8
  214.7 1.0 bitcast_add_fusion.8
  215.7 28.6 %all-gather.6.cloned.1.call-done = f32[256,64,128]{2,1,0:T(8,128)} async-done(((f32[4,64,128]{2,1,0:T(8,128)}), f32[256,64,128]{2,1,0:T(8,128)}) %all-gather.6.cloned.1.call-update) | async-done | bytes 8388624 | tf_op jit(solution)/shard_map/all_gather | solution.py:11
  244.4 94.1 %while.53 = (s32[]{:T(128)}, bf16[4,512,64]{1,2,0:T(8,128)(2,1)}, bf16[4,512,64]{1,2,0:T(8,128)(2,1)}, f32[4,512,128]{2,1,0:T(8,128)}, f32[4,512,128]{2,1,0:T(8,...) while((s32[]{:T(128)}, bf16[4,512,64]{1,2,0:T(8,128)(2,1)}, ...), condition=%wide.region_20.21_spmd.clone.clone.clone, body=%wide.region_9.20_spmd.clone.clone.sunk.clone | while | flops 1460261376 | bytes 12009441 | solution.py:125
  245.4 2.3 fusion.179
  248.4 1.9 fusion.183
  251.4 1.3 multiply_reduce_fusion.3
  252.7 1.0 fusion.188
  256.3 1.3 dynamic_update_slice.54
  257.7 2.6 fusion.184
  261.3 1.3 fusion.186
  263.3 3.3 fusion.182
  266.6 1.3 dynamic_update_slice.53
  268.9 2.3 fusion.179
  271.9 1.9 fusion.183
  274.9 1.3 multiply_reduce_fusion.3
  276.3 1.0 fusion.188
  279.8 1.3 dynamic_update_slice.54
  281.3 2.6 fusion.184
  284.9 1.3 fusion.186
  286.8 3.3 fusion.182
  290.1 1.3 dynamic_update_slice.53
  292.4 2.3 fusion.179
  295.5 1.9 fusion.183
  298.4 1.3 multiply_reduce_fusion.3
  299.8 1.0 fusion.188
  303.3 1.3 dynamic_update_slice.54
  304.8 2.6 fusion.184
  308.3 1.3 fusion.186
  310.3 3.3 fusion.182
  313.6 1.3 dynamic_update_slice.53
  315.9 2.3 fusion.179
  319.0 1.9 fusion.183
  321.9 1.3 multiply_reduce_fusion.3
  323.3 1.0 fusion.188
  326.8 1.3 dynamic_update_slice.54
  328.3 2.6 fusion.184
  331.9 1.3 fusion.186
  333.8 3.3 fusion.182
  337.1 1.3 dynamic_update_slice.53
  338.5 2.0 reduce_sum.94
  340.6 2.0 reduce_sum.95
  342.6 1.8 copy.43
  344.4 1.8 copy.44
  346.2 116.1 %reduce-scatter.3.cloned.1.call-done = f32[32,128]{1,0:T(8,128)} async-done(((f32[512,128]{1,0:T(8,128)}), f32[32,128]{1,0:T(8,128)}) %reduce-scatter.3.cloned.1.call-update) | async-done | bytes 16400 | tf_op jit(solution)/shard_map/reduce_scatter | solution.py:151
  462.3 64.8 %reduce-scatter.5.cloned.1.call-done = f32[32,128]{1,0:T(8,128)} async-done(((f32[512,128]{1,0:T(8,128)}), f32[32,128]{1,0:T(8,128)}) %reduce-scatter.5.cloned.1.call-update) | async-done | bytes 16400 | tf_op jit(solution)/shard_map/reduce_scatter | solution.py:152
  (234 shorter events, 89.8 us)
Async XLA Ops:
  7.2 142.8 %all-gather.8.cloned.1.call-start = ((), (), s32[]{:S(2)}) async-start(), calls=%async_computation.5 | async-start | bytes 8519680 | tf_op jit(solution)/shard_map/all_gather | solution.py:11
  19.0 225.3 %all-gather.6.cloned.1.call-start = ((), (), s32[]{:S(2)}) async-start(), calls=%async_computation.4 | async-start | bytes 8519680 | tf_op jit(solution)/shard_map/all_gather | solution.py:11
  22.9 439.4 %reduce-scatter.3.cloned.1.call-start = ((), (), s32[]{:S(2)}) async-start(), calls=%async_computation.2 | async-start | bytes 278528 | tf_op jit(solution)/shard_map/reduce_scatter | solution.py:151
  340.5 186.6 %reduce-scatter.5.cloned.1.call-start = ((), (), s32[]{:S(2)}) async-start(), calls=%async_computation.3 | async-start | bytes 278528 | tf_op jit(solution)/shard_map/reduce_scatter | solution.py:152
Sparse Core Ops, SparseCore 0:
  19.1 117.1 all-gather.7
  140.6 103.7 all-gather.5
  340.6 121.6 reduce-scatter.2
  466.5 60.6 reduce-scatter.4
where the time goes:
time: 538 us; the launch traced here: 534 us
  waiting for transfers between devices  210 us (39%)
  blocking collectives  119 us (22%)
  other arithmetic  89.2 us (17%)
  matrix products  71.1 us (13%)
  local copies, waits for them, and re-layouts  26.6 us (5%)
  between operations  15.8 us (3%)
    unnamed x1, blocking collectives  119 us
    reduce_scatter x1, waiting for transfers between devices, shards(): lax.psum_scatter(jnp.sum(head_wgrad, axis=0), 'head', scatter_dimension=0...  116 us
    reduce_scatter x1, waiting for transfers between devices, shards(): lax.psum_scatter(jnp.sum(head_rgrad, axis=0), 'head', scatter_dimension=0...  64.8 us
    add x63, other arithmetic, combine(): latter[0][:, None, None] * earlier[1] + latter[1]  62.8 us
    all_gather x2, waiting for transfers between devices, carried_in(): gathered = jax.tree.map(lambda a: lax.all_gather(a, axis), part)  28.6 us
    dot_general x4, matrix products, per_head(): jnp.dot(weighted * step_rate[None, :], x_f, precision=highest)  13.3 us
  transfers between devices with their start and end apart: 4, of which 3 were waited for; matrix products, arithmetic and copies ran while one was open for 15% of the time, Pallas kernels for 0%

commit v1 on v0

v1 whole, which is shorter than its diff:
```python
import jax
import jax.numpy as jnp
from jax import lax
from jax.experimental import pallas as pl
from jax.experimental.pallas import tpu as pltpu
from jax.sharding import PartitionSpec as P

F32 = jnp.float32
BF16 = jnp.bfloat16
CHUNK = 128
NEG = -1e30


def split(v):
    hi = v.astype(BF16)
    return hi, (v - hi.astype(F32)).astype(BF16)


def mm(a, b, ca, cb):
    return lax.dot_general(a, b, (((ca,), (cb,)), ((), ())), preferred_element_type=F32)


def mm_exact(a, b, ca, cb):
    return lax.dot_general(
        a, b, (((ca,), (cb,)), ((), ())),
        precision=lax.Precision.HIGHEST, preferred_element_type=F32,
    )


def iota(shape, dim):
    return lax.broadcasted_iota(jnp.int32, shape, dim)


def records_at(len_ref, pos):
    start = jnp.int32(0)
    total = (pos >= start).astype(jnp.int32)
    for k in range(len_ref.shape[0] - 1):
        start = start + len_ref[k]
        total = total + (pos >= start).astype(jnp.int32)
    return total


def scalar_record(len_ref, pos):
    start = jnp.int32(0)
    total = jnp.where(pos >= start, 1, 0)
    for k in range(len_ref.shape[0] - 1):
        start = start + len_ref[k]
        total = total + jnp.where(pos >= start, 1, 0)
    return total


def running_sums(rows):
    heads, steps = rows.shape
    chunks = steps // CHUNK
    stacked = jnp.concatenate([rows[:, q * CHUNK:(q + 1) * CHUNK] for q in range(chunks)], axis=0)
    tri = (iota((CHUNK, CHUNK), 0) <= iota((CHUNK, CHUNK), 1)).astype(F32)
    sums = mm_exact(stacked, tri, 1, 0)
    return [sums[q * heads:(q + 1) * heads, :] for q in range(chunks)]


def block_rows(len_ref, offset, ld, dt):
    heads, steps = ld.shape
    parts = running_sums(ld)
    total = jnp.zeros((heads, 1), F32)
    cums = []
    for part in parts:
        cums.append(part + total)
        total = total + part[:, CHUNK - 1:CHUNK]
    cum = jnp.concatenate(cums, axis=1)
    rec = records_at(len_ref, offset + iota((1, steps), 1))
    last = scalar_record(len_ref, offset + steps - 1)
    prev = scalar_record(len_ref, offset - 1)
    enter = jnp.exp(jnp.where(rec == prev, cum, NEG))
    leave = jnp.exp(jnp.where(rec == last, total - cum, NEG))
    keep = jnp.exp(jnp.where(last == prev, total, NEG))
    return enter, leave, keep


def lanes_of(cols, first, heads):
    rows = cols.shape[0]
    low = iota((rows, 128), 1) < 64
    out = []
    for h in range(0, heads, 2):
        a = cols[:, first + h:first + h + 1]
        b = cols[:, first + h + 1:first + h + 2]
        out.append(jnp.where(low, a, b))
    return jnp.concatenate(out, axis=1)


def state_terms(len_ref, off_ref, ld_ref, dt_ref, w_ref, r_ref, x_ref, g_ref, pay_ref):
    heads, steps = ld_ref.shape
    offset = off_ref[0]
    dt = dt_ref[...]
    enter, leave, keep = block_rows(len_ref, offset, ld_ref[...], dt)
    stack = jnp.concatenate([leave * dt, enter], axis=0)
    xs, gs = [], []
    for q in range(steps // CHUNK):
        rows = pl.ds(q * CHUNK, CHUNK)
        cols = jnp.transpose(stack[:, q * CHUNK:(q + 1) * CHUNK])
        xs.append(x_ref[rows, :].astype(F32) * lanes_of(cols, 0, heads))
        gs.append(g_ref[rows, :].astype(F32) * lanes_of(cols, heads, heads))
    x_hi, x_lo = split(jnp.concatenate(xs, axis=0))
    g_hi, g_lo = split(jnp.concatenate(gs, axis=0))
    w = w_ref[...]
    r = r_ref[...]
    fresh = mm(w, x_hi, 0, 0) + mm(w, x_lo, 0, 0)
    back = mm(r, g_hi, 0, 0) + mm(r, g_lo, 0, 0)
    low = iota((32, 128), 1) < 64
    for half in range(2):
        lanes = slice(128 * half, 128 * half + 128)
        for i in range(4):
            rows = slice(32 * i, 32 * i + 32)
            pay_ref[pl.ds(512 * half + i, 32, stride=16), :] = fresh[rows, lanes]
            pay_ref[pl.ds(512 * half + 4 + i, 32, stride=16), :] = back[rows, lanes]
        pair = jnp.where(low, keep[2 * half:2 * half + 1, :], keep[2 * half + 1:2 * half + 2, :])
        pay_ref[pl.ds(512 * half + 8, 32, stride=16), :] = pair


def scan_blocks(in_ref, out_ref):
    blocks = in_ref.shape[0] // 16
    forward = iota((8, 128), 0) < 4
    carry = jnp.zeros((8, 128), F32)
    held = []
    for j in range(blocks):
        held.append(carry)
        carry = carry * in_ref[16 * j + 8:16 * j + 9, :] + in_ref[16 * j:16 * j + 8, :]
    carry = jnp.zeros((8, 128), F32)
    for j in range(blocks - 1, -1, -1):
        out_ref[8 * j:8 * j + 8, :] = jnp.where(forward, held[j], carry)
        carry = carry * in_ref[16 * j + 8:16 * j + 9, :] + in_ref[16 * j:16 * j + 8, :]


def read_states(st_ref):
    both = []
    for kind in range(2):
        halves = []
        for half in range(2):
            halves.append(jnp.concatenate(
                [st_ref[pl.ds(256 * half + 4 * kind + i, 32, stride=8), :] for i in range(4)],
                axis=0))
        both.append(jnp.concatenate(halves, axis=1))
    return both


def local_part(len_ref, off_ref, ld_ref, dt_ref, w_ref, r_ref, x_ref, g_ref,
               y_ref, p_ref, wl_ref, rl_ref, xh_ref, xl_ref, gh_ref, gl_ref):
    heads, steps = ld_ref.shape
    chunks = steps // CHUNK
    offset = off_ref[0]
    ld = ld_ref[...]
    dt_all = dt_ref[...]
    enter_b, leave_b, _ = block_rows(len_ref, offset, ld, dt_all)
    parts = running_sums(ld)
    low = iota((CHUNK, 128), 1) < 64
    causal = iota((CHUNK, CHUNK), 1) <= iota((CHUNK, CHUNK), 0)
    saved = []
    for q in range(chunks):
        rows = pl.ds(q * CHUNK, CHUNK)
        span = slice(q * CHUNK, (q + 1) * CHUNK)
        first = offset + q * CHUNK
        cum = parts[q]
        total = cum[:, CHUNK - 1:CHUNK]
        dt = dt_all[:, span]
        rec_row = records_at(len_ref, first + iota((1, CHUNK), 1))
        rec_col = records_at(len_ref, first + iota((CHUNK, 1), 0))
        last = scalar_record(len_ref, first + CHUNK - 1)
        prev = scalar_record(len_ref, first - 1)
        enter = jnp.exp(jnp.where(rec_row == prev, cum, NEG))
        leave = jnp.exp(jnp.where(rec_row == last, total - cum, NEG))
        keep = jnp.exp(jnp.where(last == prev, total, NEG))
        stack = jnp.concatenate(
            [cum, enter, leave, leave * dt, leave_b[:, span] * dt, enter_b[:, span]], axis=0)
        cols = jnp.transpose(stack)
        x = x_ref[rows, :]
        g = g_ref[rows, :]
        xf = x.astype(F32)
        gf = g.astype(F32)
        xb_hi, xb_lo = split(xf * lanes_of(cols, 4 * heads, heads))
        gb_hi, gb_lo = split(gf * lanes_of(cols, 5 * heads, heads))
        xh_ref[rows, :] = xb_hi
        xl_ref[rows, :] = xb_lo
        gh_ref[rows, :] = gb_hi
        gl_ref[rows, :] = gb_lo
        enter_lanes = lanes_of(cols, heads, heads)
        leave_lanes = lanes_of(cols, 2 * heads, heads)
        xc = split(xf * lanes_of(cols, 3 * heads, heads))
        gc = split(gf * enter_lanes)
        w = w_ref[rows, :]
        r = r_ref[rows, :]
        fresh = mm(w, xc[0], 0, 0) + mm(w, xc[1], 0, 0)
        back = mm(r, gc[0], 0, 0) + mm(r, gc[1], 0, 0)
        keep_row = jnp.concatenate([
            jnp.where(iota((1, 128), 1) < 64, keep[h:h + 1, :], keep[h + 1:h + 2, :])
            for h in range(0, heads, 2)], axis=1)
        inside = causal & (rec_row == rec_col)
        scores = mm(r, w, 1, 1)
        total_e = jnp.zeros((CHUNK, CHUNK), F32)
        y_parts, p_parts = [], []
        for h in range(heads):
            pair = slice(128 * (h // 2), 128 * (h // 2) + 128)
            x_pair = x[:, pair]
            g_pair = g[:, pair]
            mine = low if h % 2 == 0 else ~low
            decays = jnp.exp(jnp.where(inside, cols[:, h:h + 1] - cum[h:h + 1, :], NEG))
            weighted = scores * decays
            dt_row = dt[h:h + 1, :]
            a_hi, a_lo = split(weighted * dt_row)
            y_parts.append(mm(a_hi, x_pair, 1, 0) + mm(a_lo, x_pair, 1, 0))
            b_hi, b_lo = split(weighted)
            p_parts.append(mm(b_hi, g_pair, 0, 0) + mm(b_lo, g_pair, 0, 0))
            g_mine = jnp.where(mine, gf[:, pair], 0.0).astype(BF16)
            total_e = total_e + decays * dt_row * mm(g_mine, x_pair, 1, 1)
        y = jnp.concatenate([jnp.where(low, y_parts[h], y_parts[h + 1]) for h in range(0, heads, 2)], axis=1)
        p = jnp.concatenate([jnp.where(low, p_parts[h], p_parts[h + 1]) for h in range(0, heads, 2)], axis=1)
        e_hi, e_lo = split(total_e)
        wl = mm(e_hi, r, 0, 0) + mm(e_lo, r, 0, 0)
        rl = mm(e_hi, w, 1, 0) + mm(e_lo, w, 1, 0)
        saved.append((rows, y, p, wl, rl, xc, gc, w, r, fresh, back, keep_row, enter_lanes, leave_lanes))
    state = None
    for q in range(chunks):
        rows, y, p, wl, rl, xc, gc, w, r, fresh, back, keep_row, enter_lanes, leave_lanes = saved[q]
        if state is not None:
            s_hi, s_lo = split(state)
            y = y + enter_lanes * (mm(r, s_hi, 1, 0) + mm(r, s_lo, 1, 0))
            rl = rl + (mm(gc[0], s_hi, 1, 1) + mm(gc[0], s_lo, 1, 1) + mm(gc[1], s_hi, 1, 1))
            state = state * keep_row + fresh
        else:
            state = fresh
        y_ref[rows, :] = y
        rl_ref[rows, :] = rl
    future = None
    for q in range(chunks - 1, -1, -1):
        rows, y, p, wl, rl, xc, gc, w, r, fresh, back, keep_row, enter_lanes, leave_lanes = saved[q]
        if future is not None:
            f_hi, f_lo = split(future)
            p = p + leave_lanes * (mm(w, f_hi, 1, 0) + mm(w, f_lo, 1, 0))
            wl = wl + (mm(xc[0], f_hi, 1, 1) + mm(xc[0], f_lo, 1, 1) + mm(xc[1], f_hi, 1, 1))
            future = future * keep_row + back
        else:
            future = back
        p_ref[rows, :] = p
        wl_ref[rows, :] = wl


def shared_grads(st_ref, wl_ref, rl_ref, xh_ref, xl_ref, gh_ref, gl_ref, out_ref):
    steps = wl_ref.shape[0]
    incoming, future = read_states(st_ref)
    s_hi, s_lo = split(incoming)
    f_hi, f_lo = split(future)
    xh = xh_ref[...]
    gh = gh_ref[...]
    w = wl_ref[...] + mm(xh, f_hi, 1, 1) + mm(xh, f_lo, 1, 1) + mm(xl_ref[...], f_hi, 1, 1)
    r = rl_ref[...] + mm(gh, s_hi, 1, 1) + mm(gh, s_lo, 1, 1) + mm(gl_ref[...], s_hi, 1, 1)
    share = steps // out_ref.shape[0]
    out_ref[:, 0:share, :] = w.reshape(out_ref.shape[0], share, w.shape[1])
    out_ref[:, share:2 * share, :] = r.reshape(out_ref.shape[0], share, r.shape[1])


def finish(len_ref, off_ref, ld_ref, dt_ref, w_ref, r_ref, x_ref, g_ref, y_ref, p_ref, st_ref,
           out_ref, xg_ref, sg_ref, dg_ref):
    heads, steps = ld_ref.shape
    chunks = steps // CHUNK
    offset = off_ref[0]
    ld = ld_ref[...]
    dt = dt_ref[...]
    enter, leave, keep = block_rows(len_ref, offset, ld, dt)
    incoming, future = read_states(st_ref)
    s_hi, s_lo = split(incoming)
    f_hi, f_lo = split(future)
    width = x_ref.shape[1]
    pick = (iota((8, width), 1) // 64 == iota((8, width), 0)).astype(F32)
    stack = jnp.concatenate([enter, leave, dt, dt], axis=0)
    p_rows, ql_rows, qs_rows = [], [], []
    for q in range(chunks):
        rows = pl.ds(q * CHUNK, CHUNK)
        cols = jnp.transpose(stack[:, q * CHUNK:(q + 1) * CHUNK])
        r = r_ref[rows, :]
        w = w_ref[rows, :]
        y = y_ref[rows, :] + lanes_of(cols, 0, heads) * (mm(r, s_hi, 1, 0) + mm(r, s_lo, 1, 0))
        near = p_ref[rows, :]
        far = lanes_of(cols, heads, heads) * (mm(w, f_hi, 1, 0) + mm(w, f_lo, 1, 0))
        out_ref[rows, :] = y.astype(BF16)
        xg_ref[rows, :] = (lanes_of(cols, 2 * heads, heads) * (near + far)).astype(BF16)
        xf = x_ref[rows, :].astype(F32)
        p_rows.append(mm_exact(pick, g_ref[rows, :].astype(F32) * y, 1, 1)[0:heads, :])
        ql_rows.append(mm_exact(pick, xf * near, 1, 1)[0:heads, :])
        qs_rows.append(mm_exact(pick, xf * far, 1, 1)[0:heads, :])
    both = jnp.sum((incoming * future).reshape(16, 8, width), axis=0)
    cross = keep * jnp.sum(mm_exact(pick, both, 1, 1), axis=1, keepdims=True)[0:heads, :]
    ql = jnp.concatenate(ql_rows, axis=1) * dt
    qs = jnp.concatenate(qs_rows, axis=1) * dt
    pt = jnp.concatenate(p_rows, axis=1)
    sg_ref[...] = ql + qs
    diff = pt - ql
    d_in = running_sums(diff)
    q_in = running_sums(qs)
    d_tot = [d[:, CHUNK - 1:CHUNK] for d in d_in]
    later = jnp.zeros((heads, 1), F32)
    tails = [None] * chunks
    for q in range(chunks - 1, -1, -1):
        span = slice(q * CHUNK, (q + 1) * CHUNK)
        later = later + d_tot[q]
        tails[q] = later - d_in[q] + diff[:, span]
    before = cross
    for q in range(chunks):
        span = slice(q * CHUNK, (q + 1) * CHUNK)
        total = tails[q] + before + q_in[q] - qs[:, span]
        dg_ref[:, span] = ld[:, span] * total
        before = before + q_in[q][:, CHUNK - 1:CHUNK]


def add_heads(in_ref, w_ref, r_ref):
    total = jnp.sum(in_ref[...], axis=0)
    share = w_ref.shape[0]
    w_ref[...] = total[0:share, :]
    r_ref[...] = total[share:2 * share, :]


def call(kernel, outs, args, name, flops=0, seconds_bytes=0):
    smem = pl.BlockSpec(memory_space=pltpu.SMEM)
    vmem = pl.BlockSpec(memory_space=pltpu.VMEM)
    return pl.pallas_call(
        kernel,
        out_shape=outs,
        in_specs=[smem if a.dtype == jnp.int32 else vmem for a in args],
        out_specs=jax.tree.map(lambda _: vmem, outs),
        compiler_params=pltpu.CompilerParams(vmem_limit_bytes=40 * 1024 * 1024),
        cost_estimate=pl.CostEstimate(flops=flops, bytes_accessed=seconds_bytes, transcendentals=0),
        name=name,
    )(*args)


def shards(inputs, write_map, read_map, step_scale, log_decay, lengths, out_grad):
    steps, width = inputs.shape
    heads = step_scale.shape[0]
    state = write_map.shape[1]
    blocks = lax.axis_size("ctx")
    groups = lax.axis_size("head")
    share = steps // groups
    sds = jax.ShapeDtypeStruct
    offset = (lax.axis_index("ctx") * steps).astype(jnp.int32).reshape(1)
    common = (lengths, offset, log_decay, step_scale, write_map, read_map, inputs, out_grad)
    pay = call(state_terms, sds((blocks * 16, 128), F32), common, "state_terms", 200_000_000, 2_000_000)
    got = lax.all_to_all(pay.reshape(blocks, 16, 128), "ctx", 0, 0)
    y, p, wl, rl, xh, xl, gh, gl = call(
        local_part,
        [sds((steps, width), F32), sds((steps, width), F32), sds((steps, state), F32), sds((steps, state), F32)]
        + [sds((steps, width), BF16)] * 4,
        common, "local_part", 4_000_000_000, 20_000_000)
    scanned = call(scan_blocks, sds((blocks * 8, 128), F32), (got.reshape(blocks * 16, 128),), "scan_blocks", 1_000_000, 1_000_000)
    states = lax.all_to_all(scanned.reshape(blocks, 8, 128), "ctx", 0, 0).reshape(blocks * 8, 128)
    terms = call(shared_grads, sds((groups, 2 * share, state), F32), (states, wl, rl, xh, xl, gh, gl),
                 "shared_grads", 200_000_000, 2_000_000)
    summed = lax.all_to_all(terms, "head", 0, 0)
    outputs, input_grad, step_grad, decay_grad = call(
        finish,
        [sds((steps, width), BF16), sds((steps, width), BF16), sds((heads, steps), F32), sds((heads, steps), F32)],
        common + (y, p, states), "finish", 4_000_000_000, 20_000_000)
    write_grad, read_grad = call(
        add_heads, [sds((share, state), F32), sds((share, state), F32)], (summed,), "add_heads", 1_000_000, 1_000_000)
    return (outputs, input_grad, write_grad, read_grad, step_grad, decay_grad)


def solution(mesh):
    placed = (
        P("ctx", "head"),
        P("ctx", None),
        P("ctx", None),
        P("head", "ctx"),
        P("head", "ctx"),
        P(),
        P("ctx", "head"),
    )
    return jax.shard_map(
        shards,
        mesh=mesh,
        in_specs=placed,
        out_specs=(
            P("ctx", "head"),
            P("ctx", "head"),
            P(("ctx", "head"), None),
            P(("ctx", "head"), None),
            P("head", "ctx"),
            P("head", "ctx"),
        ),
        check_vma=False,
    )
```

time: 538 us -> 99.3 us (0.18)
  waiting for transfers between devices: 210 us -> 19.8 us
  blocking collectives: 119 us -> 28.6 us
  other arithmetic: 89.2 us -> 0 us
  matrix products: 71.1 us -> 0 us
  starting transfers between devices: 0.16 us -> 29.6 us
  local copies, waits for them, and re-layouts: 26.6 us -> 5.89 us
  between operations: 15.8 us -> 0.74 us
  Pallas kernels: 0 us -> 14.1 us
    reduce_scatter x2 -> x0, waiting for transfers between devices: 181 us -> none  [the longest x1 116 us: shards(): lax.psum_scatter(jnp.sum(head_wgrad, axis=0), 'head', scatter_dimension=0...]
    unnamed x1 -> x0, blocking collectives: 119 us -> none
    dot_general x47 -> x0, matrix products: 71.1 us -> none  [the longest x4 13.3 us: per_head(): jnp.dot(weighted * step_rate[None, :], x_f, precision=highest)]
    add x64 -> x0, other arithmetic: 62.8 us -> none  [the longest x63 62.8 us: combine(): latter[0][:, None, None] * earlier[1] + latter[1]]
    all_to_all x0 -> x2, starting transfers between devices: none -> 29.6 us  [the longest x1 23.5 us: shards(): summed = lax.all_to_all(terms, 'head', 0, 0)]
    all_to_all x0 -> x1, blocking collectives: none -> 28.6 us  [shards(): got = lax.all_to_all(pay.reshape(blocks, 16, 128), 'ctx', 0, 0)]
    all_gather x2 -> x0, waiting for transfers between devices: 28.6 us -> none  [carried_in(): gathered = jax.tree.map(lambda a: lax.all_gather(a, axis), part)]
    all_to_all x0 -> x2, waiting for transfers between devices: none -> 19.8 us  [the longest x1 13.3 us: shards(): summed = lax.all_to_all(terms, 'head', 0, 0)]
  transfers between devices with their start and end apart: 4 -> 2, of which waited for: 3 -> 2; matrix products, arithmetic and copies ran while one was open for 15% -> 0% of each run, Pallas kernels for 0% -> 9%
where the time goes in v1:
time: 99.3 us; the launch traced here: 98.8 us
  starting transfers between devices  29.6 us (30%)
  blocking collectives  28.6 us (29%)
  waiting for transfers between devices  19.8 us (20%)
  Pallas kernels  14.1 us (14%)
  local copies, waits for them, and re-layouts  5.89 us (6%)
    all_to_all x1, blocking collectives, shards(): got = lax.all_to_all(pay.reshape(blocks, 16, 128), 'ctx', 0, 0)  28.6 us
    all_to_all x1, starting transfers between devices, shards(): summed = lax.all_to_all(terms, 'head', 0, 0)  23.5 us
    pallas_call x6, Pallas kernels, call(): pl.pallas_call(kernel, out_shape=outs, in_specs=[smem if a.dtype == jnp.i...  14.1 us
    all_to_all x1, waiting for transfers between devices, shards(): summed = lax.all_to_all(terms, 'head', 0, 0)  13.3 us
    all_to_all x1, waiting for transfers between devices, shards(): lax.all_to_all(scanned.reshape(blocks, 8, 128), 'ctx', 0, 0)  6.53 us
    all_to_all x1, starting transfers between devices, shards(): lax.all_to_all(scanned.reshape(blocks, 8, 128), 'ctx', 0, 0)  6.1 us
    unnamed x28, local copies, waits for them, and re-layouts  5.89 us
  transfers between devices with their start and end apart: 2, of which 2 were waited for; matrix products, arithmetic and copies ran while one was open for 0% of the time, Pallas kernels for 9%

profile of v1, /device:TPU:1, one launch (start us, length us, event | category | flops | bytes accessed | tf_op | source)
XLA Modules:
  0.0 98.8 jit_solution(7327500750459348821)
XLA Ops:
  0.6 0.0 copy-start.8
  0.6 0.0 copy-start.11
  0.7 0.7 copy-done.8
  1.3 0.0 copy-done.11
  1.3 0.0 copy-start
  1.3 0.9 copy-done
  2.3 0.0 copy-start.2
  2.3 0.9 copy-done.2
  3.2 0.0 copy-start.4
  3.2 0.9 copy-done.4
  4.1 0.0 copy-start.6
  4.1 0.9 copy-done.6
  5.0 0.0 copy-start.9
  5.0 0.7 copy-done.9
  5.7 2.1 %state_terms.1 = f32[1024,128]{1,0:T(8,128)S(1)} custom-call(s32[4]{0:T(128)S(1)} %copy-done.11, s32[1]{0:T(128)} %bitcast.off_ref, f32[4,512]{1,0:T(4,128)S(1)} %copy-done.8, f32[4,512]{1,0:T(4,128)S(1)} %copy-done.9, bf16[512,128]{1,0:T(8,128)(2,1)S(1)} %copy-done.4, bf16[512,128]{1,0:T(8,128)(2,1)S(1)} %copy-done.6, bf16[512,256]{1,0:T(8,128)(2,1)S(1)} %copy-done, ...), custom_call_target="tpu_custom_call" | custom-call | flops 200000000 | bytes 2000000 | tf_op jit(solution)/shard_map/state_terms/pallas_call | solution.py:322
  7.8 28.6 %all_to_all.15 = f32[64,16,128]{2,1,0:T(8,128)S(1)} all-to-all(f32[64,16,128]{2,1,0:T(8,128)S(1)} %bitcast.6), channel_id=1, replica_groups=mesh['ctx'=64,'head'=16] {'ctx'}, dimensions={0} | all-to-all | bytes 1048576 | tf_op jit(solution)/shard_map/all_to_all | solution.py:344
  36.5 0.0 copy-start.5
  36.5 0.0 copy-start.7
  36.5 0.0 copy-start.10
  36.5 0.9 scan_blocks.1
  37.4 0.0 copy-start.1
  37.4 0.0 copy-start.3
  37.4 6.1 %all-to-all-start.1 = ((f32[64,8,128]{2,1,0:T(8,128)}), f32[64,8,128]{2,1,0:T(8,128)S(1)}, u32[]{:S(2)}, u32[]{:S(2)}) async-start(f32[64,8,128]{2,1,0:T(8,128)} %bitcast.3), calls=%async_computation.1 | async-start | bytes 524288 | tf_op jit(solution)/shard_map/all_to_all | solution.py:351
  43.5 0.0 copy-done.5
  43.5 0.0 copy-done.7
  43.5 0.0 copy-done.10
  43.5 0.0 copy-done.1
  43.5 0.0 copy-done.3
  43.5 5.1 %local_part.1 = (f32[512,256]{1,0:T(8,128)S(1)}, f32[512,256]{1,0:T(8,128)S(1)}, f32[512,128]{1,0:T(8,128)S(1)}, f32[512,128]{1,0:T(8,128)S(1)}, bf16[512,256]{1...) custom-call(s32[4]{0:T(128)S(1)} %copy-done.11, ...), custom_call_target="tpu_custom_call" | custom-call | flops 4000000000 | bytes 20000000 | tf_op jit(solution)/shard_map/local_part/pallas_call | solution.py:322
  48.6 0.0 copy-start.12
  48.6 0.8 copy-done.12
  49.4 6.5 %all-to-all-done.1 = f32[64,8,128]{2,1,0:T(8,128)S(1)} async-done(((f32[64,8,128]{2,1,0:T(8,128)}), f32[64,8,128]{2,1,0:T(8,128)S(1)}, u32[]{:S(2)}, u32[]{:S(2)}) %all-to-all-start.1) | async-done | bytes 262176 | tf_op jit(solution)/shard_map/all_to_all | solution.py:351
  55.9 1.4 %shared_grads.1 = f32[16,64,128]{2,1,0:T(8,128)} custom-call(f32[512,128]{1,0:T(8,128)S(1)} %bitcast.7, f32[512,128]{1,0:T(8,128)S(1)} %get-tuple-element.24.wl_ref, f32[512,128]{1,0:T(8,128)S(1)} %get-tuple-element.25.rl_ref, bf16[512,256]{1,0:T(8,128)(2,1)S(1)} %get-tuple-element.26.xh_ref, bf16[512,256]{1,0:T(8,128)(2,1)S(1)} %get-tuple-element.27.xl_ref, ...), custom_call_target="tpu_custom_call" | custom-call | flops 200000000 | bytes 2000000 | tf_op jit(solution)/shard_map/shared_grads/pallas_call | solution.py:322
  57.3 0.0 copy-start.13
  57.3 23.5 %all-to-all-start.2 = ((f32[16,64,128]{2,1,0:T(8,128)}), f32[16,64,128]{2,1,0:T(8,128)S(1)}, u32[]{:S(2)}, u32[]{:S(2)}) async-start(f32[16,64,128]{2,1,0:T(8,128)} %shared_grads.1), calls=%async_computation.2 | async-start | bytes 1048576 | tf_op jit(solution)/shard_map/all_to_all | solution.py:354
  80.8 0.0 copy-done.13
  80.8 4.0 %finish.1 = (bf16[512,256]{1,0:T(8,128)(2,1)}, bf16[512,256]{1,0:T(8,128)(2,1)}, f32[4,512]{1,0:T(4,128)}, f32[4,512]{1,0:T(4,128)}) custom-call(s32[4]{0:T(128)S(1)} %copy-done.11, s32[1]{0:T(128)} %bitcast.off_ref, f32[4,512]{1,0:T(4,128)S(1)} %copy-done.8, f32[4,512]{1,0:T(4,128)S(1)} %copy-done.10, bf16[512,128]{1,0:T(8,128)(2,1)S(1)} %copy-done.5, ...), custom_call_target="tpu_custom_call" | custom-call | flops 4000000000 | bytes 20000000 | tf_op jit(solution)/shard_map/finish/pallas_call | solution.py:322
  84.8 13.3 %all-to-all-done.2.in_ref = f32[16,64,128]{2,1,0:T(8,128)S(1)} async-done(((f32[16,64,128]{2,1,0:T(8,128)}), f32[16,64,128]{2,1,0:T(8,128)S(1)}, u32[]{:S(2)}, u32[]{:S(2)}) %all-to-all-start.2) | async-done | bytes 524320 | tf_op jit(solution)/shard_map/all_to_all | solution.py:354
  98.1 0.6 add_heads.1
Async XLA Ops:
  0.6 0.7 copy-start.8
  0.6 0.7 copy-start.11
  1.3 1.0 copy-start
  2.3 0.9 copy-start.2
  3.2 0.9 copy-start.4
  4.1 0.9 copy-start.6
  5.0 0.7 copy-start.9
  36.5 7.0 %copy-start.5 = (bf16[512,128]{1,0:T(8,128)(2,1)S(1)}, bf16[512,128]{1,0:T(8,128)(2,1)}, u32[]{:S(2)}) copy-start(bf16[512,128]{1,0:T(8,128)(2,1)} %w_ref.5) | copy-start | bytes 393220
  36.5 7.0 %copy-start.7 = (bf16[512,128]{1,0:T(8,128)(2,1)S(1)}, bf16[512,128]{1,0:T(8,128)(2,1)}, u32[]{:S(2)}) copy-start(bf16[512,128]{1,0:T(8,128)(2,1)} %r_ref.5) | copy-start | bytes 393220
  36.5 7.0 %copy-start.10 = (f32[4,512]{1,0:T(4,128)S(1)}, f32[4,512]{1,0:T(4,128)}, u32[]{:S(2)}) copy-start(f32[4,512]{1,0:T(4,128)} %dt_ref.5) | copy-start | bytes 24580
  37.4 6.1 %copy-start.1 = (bf16[512,256]{1,0:T(8,128)(2,1)S(1)}, bf16[512,256]{1,0:T(8,128)(2,1)}, u32[]{:S(2)}) copy-start(bf16[512,256]{1,0:T(8,128)(2,1)} %x_ref.5) | copy-start | bytes 786436
  37.4 6.1 %copy-start.3 = (bf16[512,256]{1,0:T(8,128)(2,1)S(1)}, bf16[512,256]{1,0:T(8,128)(2,1)}, u32[]{:S(2)}) copy-start(bf16[512,256]{1,0:T(8,128)(2,1)} %g_ref.5) | copy-start | bytes 786436
  37.4 18.6 %all-to-all-start.1 = ((f32[64,8,128]{2,1,0:T(8,128)}), f32[64,8,128]{2,1,0:T(8,128)S(1)}, u32[]{:S(2)}, u32[]{:S(2)}) async-start(f32[64,8,128]{2,1,0:T(8,128)} %bitcast.3), calls=%async_computation.1 | async-start | bytes 524288 | tf_op jit(solution)/shard_map/all_to_all | solution.py:351
  48.6 0.8 copy-start.12
  57.3 23.5 %copy-start.13 = (f32[512,256]{1,0:T(8,128)S(1)}, f32[512,256]{1,0:T(8,128)}, u32[]{:S(2)}) copy-start(f32[512,256]{1,0:T(8,128)} %copy-done.12) | copy-start | bytes 1572868
  57.3 40.8 %all-to-all-start.2 = ((f32[16,64,128]{2,1,0:T(8,128)}), f32[16,64,128]{2,1,0:T(8,128)S(1)}, u32[]{:S(2)}, u32[]{:S(2)}) async-start(f32[16,64,128]{2,1,0:T(8,128)} %shared_grads.1), calls=%async_computation.2 | async-start | bytes 1048576 | tf_op jit(solution)/shard_map/all_to_all | solution.py:354

commit v2 on v1

--- a/solution.py
+++ b/solution.py
@@ -9,6 +9,7 @@
 BF16 = jnp.bfloat16
 CHUNK = 128
 NEG = -1e30
+PIECE = 9
 
 
 def split(v):
@@ -87,47 +88,62 @@
     return jnp.concatenate(out, axis=1)
 
 
-def state_terms(len_ref, off_ref, ld_ref, dt_ref, w_ref, r_ref, x_ref, g_ref, pay_ref):
+def state_terms(len_ref, off_ref, ld_hbm, dt_hbm, w_hbm, r_hbm, x_hbm, g_hbm, pay_ref,
+                ld_ref, dt_ref, w_ref, r_ref, x_ref, g_ref, sems):
+    copies = [
+        pltpu.make_async_copy(src, dst, sems.at[i])
+        for i, (src, dst) in enumerate((
+            (ld_hbm, ld_ref), (dt_hbm, dt_ref), (x_hbm, x_ref),
+            (w_hbm, w_ref), (g_hbm, g_ref), (r_hbm, r_ref)))
+    ]
+    for copy in copies:
+        copy.start()
+    copies[0].wait()
+    copies[1].wait()
     heads, steps = ld_ref.shape
     offset = off_ref[0]
     dt = dt_ref[...]
     enter, leave, keep = block_rows(len_ref, offset, ld_ref[...], dt)
     stack = jnp.concatenate([leave * dt, enter], axis=0)
-    xs, gs = [], []
-    for q in range(steps // CHUNK):
-        rows = pl.ds(q * CHUNK, CHUNK)
-        cols = jnp.transpose(stack[:, q * CHUNK:(q + 1) * CHUNK])
-        xs.append(x_ref[rows, :].astype(F32) * lanes_of(cols, 0, heads))
-        gs.append(g_ref[rows, :].astype(F32) * lanes_of(cols, heads, heads))
-    x_hi, x_lo = split(jnp.concatenate(xs, axis=0))
-    g_hi, g_lo = split(jnp.concatenate(gs, axis=0))
+    cols = [jnp.transpose(stack[:, q * CHUNK:(q + 1) * CHUNK]) for q in range(steps // CHUNK)]
+
+    def scaled(ref, first):
+        return split(jnp.concatenate([
+            ref[pl.ds(q * CHUNK, CHUNK), :].astype(F32) * lanes_of(cols[q], first, heads)
+            for q in range(steps // CHUNK)], axis=0))
+
+    for copy in copies[2:]:
+        copy.wait()
+    x_hi, x_lo = scaled(x_ref, 0)
     w = w_ref[...]
+    fresh = mm(w, x_hi, 0, 0) + mm(w, x_lo, 0, 0)
+    g_hi, g_lo = scaled(g_ref, heads)
     r = r_ref[...]
-    fresh = mm(w, x_hi, 0, 0) + mm(w, x_lo, 0, 0)
     back = mm(r, g_hi, 0, 0) + mm(r, g_lo, 0, 0)
     low = iota((32, 128), 1) < 64
     for half in range(2):
         lanes = slice(128 * half, 128 * half + 128)
+        base = 32 * PIECE * half
         for i in range(4):
             rows = slice(32 * i, 32 * i + 32)
-            pay_ref[pl.ds(512 * half + i, 32, stride=16), :] = fresh[rows, lanes]
-            pay_ref[pl.ds(512 * half + 4 + i, 32, stride=16), :] = back[rows, lanes]
+            pay_ref[pl.ds(base + i, 32, stride=PIECE), :] = fresh[rows, lanes]
+            pay_ref[pl.ds(base + 4 + i, 32, stride=PIECE), :] = back[rows, lanes]
         pair = jnp.where(low, keep[2 * half:2 * half + 1, :], keep[2 * half + 1:2 * half + 2, :])
-        pay_ref[pl.ds(512 * half + 8, 32, stride=16), :] = pair
+        pay_ref[pl.ds(base + 8, 32, stride=PIECE), :] = pair
 
 
 def scan_blocks(in_ref, out_ref):
-    blocks = in_ref.shape[0] // 16
+    blocks = in_ref.shape[0] // PIECE
     forward = iota((8, 128), 0) < 4
     carry = jnp.zeros((8, 128), F32)
     held = []
     for j in range(blocks):
         held.append(carry)
-        carry = carry * in_ref[16 * j + 8:16 * j + 9, :] + in_ref[16 * j:16 * j + 8, :]
+        carry = carry * in_ref[PIECE * j + 8:PIECE * j + 9, :] + in_ref[PIECE * j:PIECE * j + 8, :]
     carry = jnp.zeros((8, 128), F32)
     for j in range(blocks - 1, -1, -1):
         out_ref[8 * j:8 * j + 8, :] = jnp.where(forward, held[j], carry)
-        carry = carry * in_ref[16 * j + 8:16 * j + 9, :] + in_ref[16 * j:16 * j + 8, :]
+        carry = carry * in_ref[PIECE * j + 8:PIECE * j + 9, :] + in_ref[PIECE * j:PIECE * j + 8, :]
 
 
 def read_states(st_ref):
@@ -316,16 +332,18 @@
     r_ref[...] = total[share:2 * share, :]
 
 
-def call(kernel, outs, args, name, flops=0, seconds_bytes=0):
+def call(kernel, outs, args, name, flops=0, moved=0, scratch=(), fetched=False, limit=40):
     smem = pl.BlockSpec(memory_space=pltpu.SMEM)
     vmem = pl.BlockSpec(memory_space=pltpu.VMEM)
+    big = pl.BlockSpec(memory_space=pltpu.HBM) if fetched else vmem
     return pl.pallas_call(
         kernel,
         out_shape=outs,
-        in_specs=[smem if a.dtype == jnp.int32 else vmem for a in args],
+        in_specs=[smem if a.dtype == jnp.int32 else big for a in args],
         out_specs=jax.tree.map(lambda _: vmem, outs),
-        compiler_params=pltpu.CompilerParams(vmem_limit_bytes=40 * 1024 * 1024),
-        cost_estimate=pl.CostEstimate(flops=flops, bytes_accessed=seconds_bytes, transcendentals=0),
+        scratch_shapes=list(scratch),
+        compiler_params=pltpu.CompilerParams(vmem_limit_bytes=limit * 1024 * 1024),
+        cost_estimate=pl.CostEstimate(flops=flops, bytes_accessed=moved, transcendentals=0),
         name=name,
     )(*args)
 
@@ -340,14 +358,16 @@
     sds = jax.ShapeDtypeStruct
     offset = (lax.axis_index("ctx") * steps).astype(jnp.int32).reshape(1)
     common = (lengths, offset, log_decay, step_scale, write_map, read_map, inputs, out_grad)
-    pay = call(state_terms, sds((blocks * 16, 128), F32), common, "state_terms", 200_000_000, 2_000_000)
-    got = lax.all_to_all(pay.reshape(blocks, 16, 128), "ctx", 0, 0)
+    buffers = [pltpu.VMEM(a.shape, a.dtype) for a in common[2:]] + [pltpu.SemaphoreType.DMA((6,))]
+    pay = call(state_terms, sds((blocks * PIECE, 128), F32), common, "state_terms", 200_000_000, 2_000_000,
+               buffers, True, 60)
+    got = lax.all_to_all(pay.reshape(blocks, 1, PIECE * 128), "ctx", 0, 0)
     y, p, wl, rl, xh, xl, gh, gl = call(
         local_part,
         [sds((steps, width), F32), sds((steps, width), F32), sds((steps, state), F32), sds((steps, state), F32)]
         + [sds((steps, width), BF16)] * 4,
         common, "local_part", 4_000_000_000, 20_000_000)
-    scanned = call(scan_blocks, sds((blocks * 8, 128), F32), (got.reshape(blocks * 16, 128),), "scan_blocks", 1_000_000, 1_000_000)
+    scanned = call(scan_blocks, sds((blocks * 8, 128), F32), (got.reshape(blocks * PIECE, 128),), "scan_blocks", 1_000_000, 1_000_000)
     states = lax.all_to_all(scanned.reshape(blocks, 8, 128), "ctx", 0, 0).reshape(blocks * 8, 128)
     terms = call(shared_grads, sds((groups, 2 * share, state), F32), (states, wl, rl, xh, xl, gh, gl),
                  "shared_grads", 200_000_000, 2_000_000)

time: 99.3 us -> 90.9 us (0.915)
  local copies, waits for them, and re-layouts: 5.89 us -> 0.81 us
  starting transfers between devices: 29.6 us -> 26.8 us
  blocking collectives: 28.6 us -> 26.7 us
  Pallas kernels: 14.1 us -> 15.6 us
    unnamed x28 -> x18, local copies, waits for them, and re-layouts: 5.89 us -> 0.81 us
    all_to_all x1, blocking collectives: 28.6 us -> 26.7 us  [shards(): got = lax.all_to_all(pay.reshape(blocks, 1, PIECE * 128), 'ctx', 0, 0)]
    all_to_all x1, starting transfers between devices: 23.5 us -> 22 us  [shards(): summed = lax.all_to_all(terms, 'head', 0, 0)]
    pallas_call x6, Pallas kernels: 14.1 us -> 15.6 us  [call(): pl.pallas_call(kernel, out_shape=outs, in_specs=[smem if a.dtype == jnp.i...]
    all_to_all x1, starting transfers between devices: 6.1 us -> 4.76 us  [shards(): lax.all_to_all(scanned.reshape(blocks, 8, 128), 'ctx', 0, 0)]
  transfers between devices with their start and end apart: 2 -> 2, of which waited for: 2 -> 2; matrix products, arithmetic and copies ran while one was open for 0% -> 0% of each run, Pallas kernels for 9% -> 10%
where the time goes in v2:
time: 90.9 us; the launch traced here: 90.5 us
  starting transfers between devices  26.8 us (29%)
  blocking collectives  26.7 us (29%)
  waiting for transfers between devices  19.8 us (22%)
  Pallas kernels  15.6 us (17%)
    all_to_all x1, blocking collectives, shards(): got = lax.all_to_all(pay.reshape(blocks, 1, PIECE * 128), 'ctx', 0, 0)  26.7 us
    all_to_all x1, starting transfers between devices, shards(): summed = lax.all_to_all(terms, 'head', 0, 0)  22 us
    pallas_call x6, Pallas kernels, call(): pl.pallas_call(kernel, out_shape=outs, in_specs=[smem if a.dtype == jnp.i...  15.6 us
    all_to_all x1, waiting for transfers between devices, shards(): summed = lax.all_to_all(terms, 'head', 0, 0)  13.3 us
    all_to_all x1, waiting for transfers between devices, shards(): lax.all_to_all(scanned.reshape(blocks, 8, 128), 'ctx', 0, 0)  6.53 us
    all_to_all x1, starting transfers between devices, shards(): lax.all_to_all(scanned.reshape(blocks, 8, 128), 'ctx', 0, 0)  4.76 us
  transfers between devices with their start and end apart: 2, of which 2 were waited for; matrix products, arithmetic and copies ran while one was open for 0% of the time, Pallas kernels for 10%

profile of v2, /device:TPU:1, one launch (start us, length us, event | category | flops | bytes accessed | tf_op | source)
XLA Modules:
  0.0 90.5 jit_solution(17335510850551978893)
XLA Ops:
  0.6 3.6 %state_terms.1 = f32[576,128]{1,0:T(8,128)} custom-call(s32[4]{0:T(128)} %len_ref.5, s32[1]{0:T(128)} %bitcast.off_ref, f32[4,512]{1,0:T(4,128)} %ld_ref.3, f32[4,512]{1,0:T(4,128)} %dt_ref.3, bf16[512,128]{1,0:T(8,128)(2,1)} %w_ref.3, bf16[512,128]{1,0:T(8,128)(2,1)} %r_ref.3, bf16[512,256]{1,0:T(8,128)(2,1)} %x_ref.3, bf16[512,256]{1,0:T(8,128)(2,1)} %g_ref.3), custom_call_target="tpu_custom_call" | custom-call | flops 200000000 | bytes 2000000 | tf_op jit(solution)/shard_map/state_terms/pallas_call | solution.py:339
  4.2 26.7 %all_to_all.15 = f32[64,1,1152]{2,1,0:T(1,128)S(1)} all-to-all(f32[64,1,1152]{2,1,0:T(1,128)} %bitcast.8), channel_id=1, replica_groups=mesh['ctx'=64,'head'=16] {'ctx'}, dimensions={0} | all-to-all | bytes 589824 | tf_op jit(solution)/shard_map/all_to_all | solution.py:364
  31.0 0.0 copy-start.2
  31.0 0.0 copy-start.3
  31.0 0.0 copy-start.4
  31.0 0.0 copy-start.5
  31.0 0.0 copy-start.6
  31.0 0.9 scan_blocks.1
  31.9 0.0 copy-start
  31.9 0.0 copy-start.1
  31.9 4.8 %all-to-all-start.1 = ((f32[64,8,128]{2,1,0:T(8,128)}), f32[64,8,128]{2,1,0:T(8,128)S(1)}, u32[]{:S(2)}, u32[]{:S(2)}) async-start(f32[64,8,128]{2,1,0:T(8,128)} %bitcast.3), calls=%async_computation.1 | async-start | bytes 524288 | tf_op jit(solution)/shard_map/all_to_all | solution.py:371
  36.6 0.0 copy-done.2
  36.6 0.0 copy-done.3
  36.6 0.0 copy-done.4
  36.7 0.0 copy-done.5
  36.7 0.0 copy-done.6
  36.7 0.0 copy-done
  36.7 0.0 copy-done.1
  36.7 5.1 %local_part.1 = (f32[512,256]{1,0:T(8,128)S(1)}, f32[512,256]{1,0:T(8,128)S(1)}, f32[512,128]{1,0:T(8,128)S(1)}, f32[512,128]{1,0:T(8,128)S(1)}, bf16[512,256]{1...) custom-call(s32[4]{0:T(128)S(1)} %copy-done.6, ...), custom_call_target="tpu_custom_call" | custom-call | flops 4000000000 | bytes 20000000 | tf_op jit(solution)/shard_map/local_part/pallas_call | solution.py:339
  41.8 0.0 copy-start.7
  41.8 0.8 copy-done.7
  42.6 6.5 %all-to-all-done.1 = f32[64,8,128]{2,1,0:T(8,128)S(1)} async-done(((f32[64,8,128]{2,1,0:T(8,128)}), f32[64,8,128]{2,1,0:T(8,128)S(1)}, u32[]{:S(2)}, u32[]{:S(2)}) %all-to-all-start.1) | async-done | bytes 262176 | tf_op jit(solution)/shard_map/all_to_all | solution.py:371
  49.1 1.4 %shared_grads.1 = f32[16,64,128]{2,1,0:T(8,128)} custom-call(f32[512,128]{1,0:T(8,128)S(1)} %bitcast.6, f32[512,128]{1,0:T(8,128)S(1)} %get-tuple-element.24.wl_ref, f32[512,128]{1,0:T(8,128)S(1)} %get-tuple-element.25.rl_ref, bf16[512,256]{1,0:T(8,128)(2,1)S(1)} %get-tuple-element.26.xh_ref, bf16[512,256]{1,0:T(8,128)(2,1)S(1)} %get-tuple-element.27.xl_ref, ...), custom_call_target="tpu_custom_call" | custom-call | flops 200000000 | bytes 2000000 | tf_op jit(solution)/shard_map/shared_grads/pallas_call | solution.py:339
  50.5 0.0 copy-start.8
  50.5 22.0 %all-to-all-start.2 = ((f32[16,64,128]{2,1,0:T(8,128)}), f32[16,64,128]{2,1,0:T(8,128)S(1)}, u32[]{:S(2)}, u32[]{:S(2)}) async-start(f32[16,64,128]{2,1,0:T(8,128)} %shared_grads.1), calls=%async_computation.2 | async-start | bytes 1048576 | tf_op jit(solution)/shard_map/all_to_all | solution.py:374
  72.5 0.0 copy-done.8
  72.5 4.0 %finish.1 = (bf16[512,256]{1,0:T(8,128)(2,1)}, bf16[512,256]{1,0:T(8,128)(2,1)}, f32[4,512]{1,0:T(4,128)}, f32[4,512]{1,0:T(4,128)}) custom-call(s32[4]{0:T(128)S(1)} %copy-done.6, s32[1]{0:T(128)} %bitcast.off_ref, f32[4,512]{1,0:T(4,128)S(1)} %copy-done.4, f32[4,512]{1,0:T(4,128)S(1)} %copy-done.5, bf16[512,128]{1,0:T(8,128)(2,1)S(1)} %copy-done.2, ...), custom_call_target="tpu_custom_call" | custom-call | flops 4000000000 | bytes 20000000 | tf_op jit(solution)/shard_map/finish/pallas_call | solution.py:339
  76.5 13.3 %all-to-all-done.2.in_ref = f32[16,64,128]{2,1,0:T(8,128)S(1)} async-done(((f32[16,64,128]{2,1,0:T(8,128)}), f32[16,64,128]{2,1,0:T(8,128)S(1)}, u32[]{:S(2)}, u32[]{:S(2)}) %all-to-all-start.2) | async-done | bytes 524320 | tf_op jit(solution)/shard_map/all_to_all | solution.py:374
  89.8 0.6 add_heads.1
Async XLA Ops:
  31.0 5.7 %copy-start.2 = (bf16[512,128]{1,0:T(8,128)(2,1)S(1)}, bf16[512,128]{1,0:T(8,128)(2,1)}, u32[]{:S(2)}) copy-start(bf16[512,128]{1,0:T(8,128)(2,1)} %w_ref.3) | copy-start | bytes 393220
  31.0 5.7 %copy-start.3 = (bf16[512,128]{1,0:T(8,128)(2,1)S(1)}, bf16[512,128]{1,0:T(8,128)(2,1)}, u32[]{:S(2)}) copy-start(bf16[512,128]{1,0:T(8,128)(2,1)} %r_ref.3) | copy-start | bytes 393220
  31.0 5.7 %copy-start.4 = (f32[4,512]{1,0:T(4,128)S(1)}, f32[4,512]{1,0:T(4,128)}, u32[]{:S(2)}) copy-start(f32[4,512]{1,0:T(4,128)} %ld_ref.3) | copy-start | bytes 24580
  31.0 5.7 %copy-start.5 = (f32[4,512]{1,0:T(4,128)S(1)}, f32[4,512]{1,0:T(4,128)}, u32[]{:S(2)}) copy-start(f32[4,512]{1,0:T(4,128)} %dt_ref.3) | copy-start | bytes 24580
  31.0 5.7 %copy-start.6 = (s32[4]{0:T(128)S(1)}, s32[4]{0:T(128)}, u32[]{:S(2)}) copy-start(s32[4]{0:T(128)} %len_ref.5) | copy-start | bytes 52
  31.9 4.8 %copy-start = (bf16[512,256]{1,0:T(8,128)(2,1)S(1)}, bf16[512,256]{1,0:T(8,128)(2,1)}, u32[]{:S(2)}) copy-start(bf16[512,256]{1,0:T(8,128)(2,1)} %x_ref.3) | copy-start | bytes 786436
  31.9 4.8 %copy-start.1 = (bf16[512,256]{1,0:T(8,128)(2,1)S(1)}, bf16[512,256]{1,0:T(8,128)(2,1)}, u32[]{:S(2)}) copy-start(bf16[512,256]{1,0:T(8,128)(2,1)} %g_ref.3) | copy-start | bytes 786436
  31.9 17.2 %all-to-all-start.1 = ((f32[64,8,128]{2,1,0:T(8,128)}), f32[64,8,128]{2,1,0:T(8,128)S(1)}, u32[]{:S(2)}, u32[]{:S(2)}) async-start(f32[64,8,128]{2,1,0:T(8,128)} %bitcast.3), calls=%async_computation.1 | async-start | bytes 524288 | tf_op jit(solution)/shard_map/all_to_all | solution.py:371
  41.8 0.8 copy-start.7
  50.5 22.0 %copy-start.8 = (f32[512,256]{1,0:T(8,128)S(1)}, f32[512,256]{1,0:T(8,128)}, u32[]{:S(2)}) copy-start(f32[512,256]{1,0:T(8,128)} %copy-done.7) | copy-start | bytes 1572868
  50.5 39.3 %all-to-all-start.2 = ((f32[16,64,128]{2,1,0:T(8,128)}), f32[16,64,128]{2,1,0:T(8,128)S(1)}, u32[]{:S(2)}, u32[]{:S(2)}) async-start(f32[16,64,128]{2,1,0:T(8,128)} %shared_grads.1), calls=%async_computation.2 | async-start | bytes 1048576 | tf_op jit(solution)/shard_map/all_to_all | solution.py:374

commit v3 on v2

--- a/solution.py
+++ b/solution.py
@@ -88,48 +88,56 @@
     return jnp.concatenate(out, axis=1)
 
 
-def state_terms(len_ref, off_ref, ld_hbm, dt_hbm, w_hbm, r_hbm, x_hbm, g_hbm, pay_ref,
-                ld_ref, dt_ref, w_ref, r_ref, x_ref, g_ref, sems):
-    copies = [
-        pltpu.make_async_copy(src, dst, sems.at[i])
-        for i, (src, dst) in enumerate((
-            (ld_hbm, ld_ref), (dt_hbm, dt_ref), (x_hbm, x_ref),
-            (w_hbm, w_ref), (g_hbm, g_ref), (r_hbm, r_ref)))
-    ]
+def block_start(steps):
+    return lax.axis_index("ctx") * steps
+
+
+def state_terms(len_hbm, ld_hbm, dt_hbm, w_hbm, r_hbm, x_hbm, g_hbm, pay_hbm,
+                len_ref, ld_ref, dt_ref, w_ref, r_ref, x_ref, g_ref, pay_ref, sems):
+    pairs = ((len_hbm, len_ref), (ld_hbm, ld_ref), (dt_hbm, dt_ref), (x_hbm, x_ref),
+             (w_hbm, w_ref), (g_hbm, g_ref), (r_hbm, r_ref))
+    copies = [pltpu.make_async_copy(src, dst, sems.at[i]) for i, (src, dst) in enumerate(pairs)]
     for copy in copies:
         copy.start()
-    copies[0].wait()
-    copies[1].wait()
+    for copy in copies[:3]:
+        copy.wait()
     heads, steps = ld_ref.shape
-    offset = off_ref[0]
     dt = dt_ref[...]
-    enter, leave, keep = block_rows(len_ref, offset, ld_ref[...], dt)
+    enter, leave, keep = block_rows(len_ref, block_start(steps), ld_ref[...], dt)
     stack = jnp.concatenate([leave * dt, enter], axis=0)
     cols = [jnp.transpose(stack[:, q * CHUNK:(q + 1) * CHUNK]) for q in range(steps // CHUNK)]
-
-    def scaled(ref, first):
+    low = iota((CHUNK, 128), 1) < 64
+
+    def scaled(ref, lanes, first):
         return split(jnp.concatenate([
-            ref[pl.ds(q * CHUNK, CHUNK), :].astype(F32) * lanes_of(cols[q], first, heads)
+            ref[pl.ds(q * CHUNK, CHUNK), lanes].astype(F32)
+            * jnp.where(low, cols[q][:, first:first + 1], cols[q][:, first + 1:first + 2])
             for q in range(steps // CHUNK)], axis=0))
 
-    for copy in copies[2:]:
+    for copy in copies[3:]:
         copy.wait()
-    x_hi, x_lo = scaled(x_ref, 0)
     w = w_ref[...]
-    fresh = mm(w, x_hi, 0, 0) + mm(w, x_lo, 0, 0)
-    g_hi, g_lo = scaled(g_ref, heads)
     r = r_ref[...]
-    back = mm(r, g_hi, 0, 0) + mm(r, g_lo, 0, 0)
-    low = iota((32, 128), 1) < 64
+    half_rows = pay_ref.shape[0] // 2
+    sends = []
     for half in range(2):
         lanes = slice(128 * half, 128 * half + 128)
-        base = 32 * PIECE * half
+        base = half_rows * half
+        x_hi, x_lo = scaled(x_ref, lanes, 2 * half)
+        fresh = mm(w, x_hi, 0, 0) + mm(w, x_lo, 0, 0)
+        g_hi, g_lo = scaled(g_ref, lanes, heads + 2 * half)
+        back = mm(r, g_hi, 0, 0) + mm(r, g_lo, 0, 0)
         for i in range(4):
             rows = slice(32 * i, 32 * i + 32)
-            pay_ref[pl.ds(base + i, 32, stride=PIECE), :] = fresh[rows, lanes]
-            pay_ref[pl.ds(base + 4 + i, 32, stride=PIECE), :] = back[rows, lanes]
-        pair = jnp.where(low, keep[2 * half:2 * half + 1, :], keep[2 * half + 1:2 * half + 2, :])
+            pay_ref[pl.ds(base + i, 32, stride=PIECE), :] = fresh[rows]
+            pay_ref[pl.ds(base + 4 + i, 32, stride=PIECE), :] = back[rows]
+        pair = jnp.where(low[0:32], keep[2 * half:2 * half + 1, :], keep[2 * half + 1:2 * half + 2, :])
         pay_ref[pl.ds(base + 8, 32, stride=PIECE), :] = pair
+        span = pl.ds(base, half_rows)
+        sends.append(pltpu.make_async_copy(pay_ref.at[span], pay_hbm.at[span], sems.at[len(pairs) + half]))
+        sends[-1].start()
+    for send in sends:
+        send.wait()
 
 
 def scan_blocks(in_ref, out_ref):
@@ -158,11 +166,11 @@
     return both
 
 
-def local_part(len_ref, off_ref, ld_ref, dt_ref, w_ref, r_ref, x_ref, g_ref,
+def local_part(len_ref, ld_ref, dt_ref, w_ref, r_ref, x_ref, g_ref,
                y_ref, p_ref, wl_ref, rl_ref, xh_ref, xl_ref, gh_ref, gl_ref):
     heads, steps = ld_ref.shape
     chunks = steps // CHUNK
-    offset = off_ref[0]
+    offset = block_start(steps)
     ld = ld_ref[...]
     dt_all = dt_ref[...]
     enter_b, leave_b, _ = block_rows(len_ref, offset, ld, dt_all)
@@ -272,11 +280,11 @@
     out_ref[:, share:2 * share, :] = r.reshape(out_ref.shape[0], share, r.shape[1])
 
 
-def finish(len_ref, off_ref, ld_ref, dt_ref, w_ref, r_ref, x_ref, g_ref, y_ref, p_ref, st_ref,
+def finish(len_ref, ld_ref, dt_ref, w_ref, r_ref, x_ref, g_ref, y_ref, p_ref, st_ref,
            out_ref, xg_ref, sg_ref, dg_ref):
     heads, steps = ld_ref.shape
     chunks = steps // CHUNK
-    offset = off_ref[0]
+    offset = block_start(steps)
     ld = ld_ref[...]
     dt = dt_ref[...]
     enter, leave, keep = block_rows(len_ref, offset, ld, dt)
@@ -335,17 +343,25 @@
 def call(kernel, outs, args, name, flops=0, moved=0, scratch=(), fetched=False, limit=40):
     smem = pl.BlockSpec(memory_space=pltpu.SMEM)
     vmem = pl.BlockSpec(memory_space=pltpu.VMEM)
-    big = pl.BlockSpec(memory_space=pltpu.HBM) if fetched else vmem
+    hbm = pl.BlockSpec(memory_space=pltpu.HBM)
     return pl.pallas_call(
         kernel,
         out_shape=outs,
-        in_specs=[smem if a.dtype == jnp.int32 else big for a in args],
-        out_specs=jax.tree.map(lambda _: vmem, outs),
+        in_specs=[hbm if fetched else smem if a.dtype == jnp.int32 else vmem for a in args],
+        out_specs=jax.tree.map(lambda _: hbm if fetched else vmem, outs),
         scratch_shapes=list(scratch),
         compiler_params=pltpu.CompilerParams(vmem_limit_bytes=limit * 1024 * 1024),
         cost_estimate=pl.CostEstimate(flops=flops, bytes_accessed=moved, transcendentals=0),
         name=name,
     )(*args)
+
+
+def state_terms_call(common, blocks):
+    out = jax.ShapeDtypeStruct((blocks * PIECE, 128), F32)
+    buffers = [pltpu.SMEM(common[0].shape, common[0].dtype)]
+    buffers += [pltpu.VMEM(a.shape, a.dtype) for a in common[1:] + (out,)]
+    buffers.append(pltpu.SemaphoreType.DMA((9,)))
+    return call(state_terms, out, common, "state_terms", 200_000_000, 2_000_000, buffers, True, 60)
 
 
 def shards(inputs, write_map, read_map, step_scale, log_decay, lengths, out_grad):
@@ -356,17 +372,16 @@
     groups = lax.axis_size("head")
     share = steps // groups
     sds = jax.ShapeDtypeStruct
-    offset = (lax.axis_index("ctx") * steps).astype(jnp.int32).reshape(1)
-    common = (lengths, offset, log_decay, step_scale, write_map, read_map, inputs, out_grad)
-    buffers = [pltpu.VMEM(a.shape, a.dtype) for a in common[2:]] + [pltpu.SemaphoreType.DMA((6,))]
-    pay = call(state_terms, sds((blocks * PIECE, 128), F32), common, "state_terms", 200_000_000, 2_000_000,
-               buffers, True, 60)
+    common = (lengths, log_decay, step_scale, write_map, read_map, inputs, out_grad)
+    pay = state_terms_call(common, blocks)
+    pay, common = lax.optimization_barrier((pay, common))
     got = lax.all_to_all(pay.reshape(blocks, 1, PIECE * 128), "ctx", 0, 0)
     y, p, wl, rl, xh, xl, gh, gl = call(
         local_part,
         [sds((steps, width), F32), sds((steps, width), F32), sds((steps, state), F32), sds((steps, state), F32)]
         + [sds((steps, width), BF16)] * 4,
         common, "local_part", 4_000_000_000, 20_000_000)
+    got, wl, rl = lax.optimization_barrier((got, wl, rl))
     scanned = call(scan_blocks, sds((blocks * 8, 128), F32), (got.reshape(blocks * PIECE, 128),), "scan_blocks", 1_000_000, 1_000_000)
     states = lax.all_to_all(scanned.reshape(blocks, 8, 128), "ctx", 0, 0).reshape(blocks * 8, 128)
     terms = call(shared_grads, sds((groups, 2 * share, state), F32), (states, wl, rl, xh, xl, gh, gl),

time: 90.9 us -> 89.4 us (0.983)
  blocking collectives: 26.7 us -> 18.5 us
  starting transfers between devices: 26.8 us -> 34.6 us
  Pallas kernels: 15.6 us -> 14.3 us
    all_to_all x1, starting transfers between devices: 4.76 us -> 14.2 us  [shards(): got = lax.all_to_all(pay.reshape(blocks, 1, PIECE * 128), 'ctx', 0, 0)]
    all_to_all x1, blocking collectives: 26.7 us -> 18.5 us  [shards(): lax.all_to_all(scanned.reshape(blocks, 8, 128), 'ctx', 0, 0)]
    all_to_all x1, starting transfers between devices: 22 us -> 20.4 us  [shards(): summed = lax.all_to_all(terms, 'head', 0, 0)]
    pallas_call x6, Pallas kernels: 15.6 us -> 14.3 us  [call(): pl.pallas_call(kernel, out_shape=outs, in_specs=[hbm if fetched else smem...]
where the time goes in v3:
time: 89.4 us; the launch traced here: 89 us
  starting transfers between devices  34.6 us (39%)
  waiting for transfers between devices  19.2 us (21%)
  blocking collectives  18.5 us (21%)
  Pallas kernels  14.3 us (16%)
  local copies, waits for them, and re-layouts  1.64 us (2%)
    all_to_all x1, starting transfers between devices, shards(): summed = lax.all_to_all(terms, 'head', 0, 0)  20.4 us
    all_to_all x1, blocking collectives, shards(): lax.all_to_all(scanned.reshape(blocks, 8, 128), 'ctx', 0, 0)  18.5 us
    pallas_call x6, Pallas kernels, call(): pl.pallas_call(kernel, out_shape=outs, in_specs=[hbm if fetched else smem...  14.3 us
    all_to_all x1, starting transfers between devices, shards(): got = lax.all_to_all(pay.reshape(blocks, 1, PIECE * 128), 'ctx', 0, 0)  14.2 us
    all_to_all x1, waiting for transfers between devices, shards(): summed = lax.all_to_all(terms, 'head', 0, 0)  13.3 us
    all_to_all x1, waiting for transfers between devices, shards(): got = lax.all_to_all(pay.reshape(blocks, 1, PIECE * 128), 'ctx', 0, 0)  5.9 us
  transfers between devices with their start and end apart: 2, of which 2 were waited for; matrix products, arithmetic and copies ran while one was open for 0% of the time, Pallas kernels for 10%

profile of v3, /device:TPU:1, one launch (start us, length us, event | category | flops | bytes accessed | tf_op | source)
XLA Modules:
  0.0 89.0 jit_solution(6597439941846655524)
XLA Ops:
  0.6 0.0 copy-start.2
  0.6 0.0 copy-start.3
  0.7 3.0 %state_terms.1 = f32[576,128]{1,0:T(8,128)} custom-call(s32[4]{0:T(128)} %len_ref.1, f32[4,512]{1,0:T(4,128)} %ld_ref.1, f32[4,512]{1,0:T(4,128)} %dt_ref.1, bf16[512,128]{1,0:T(8,128)(2,1)} %w_ref.1, bf16[512,128]{1,0:T(8,128)(2,1)} %r_ref.1, bf16[512,256]{1,0:T(8,128)(2,1)} %x_ref.1, bf16[512,256]{1,0:T(8,128)(2,1)} %g_ref.1), custom_call_target="tpu_custom_call" | custom-call | flops 200000000 | bytes 2000000 | tf_op jit(solution)/shard_map/state_terms/pallas_call | solution.py:347
  3.6 0.0 copy-start
  3.6 0.0 copy-start.1
  3.7 0.0 copy-start.4
  3.7 0.0 copy-start.5
  3.7 0.0 copy-start.6
  3.7 14.2 %all-to-all-start = ((f32[64,1,1152]{2,1,0:T(1,128)}), f32[64,1,1152]{2,1,0:T(1,128)S(1)}, u32[]{:S(2)}, u32[]{:S(2)}) async-start(f32[64,1,1152]{2,1,0:T(1,128)} %bitcast.8), calls=%async_computation | async-start | bytes 589824 | tf_op jit(solution)/shard_map/all_to_all | solution.py:378
  17.9 0.0 copy-done.2
  17.9 0.0 copy-done.3
  17.9 0.0 copy-done
  17.9 0.0 copy-done.1
  17.9 0.0 copy-done.4
  17.9 0.0 copy-done.5
  17.9 0.0 copy-done.6
  17.9 5.1 %local_part.1 = (f32[512,256]{1,0:T(8,128)S(1)}, f32[512,256]{1,0:T(8,128)S(1)}, f32[512,128]{1,0:T(8,128)S(1)}, f32[512,128]{1,0:T(8,128)S(1)}, bf16[512,256]{1...) custom-call(s32[4]{0:T(128)S(1)} %copy-done.6, ...), custom_call_target="tpu_custom_call" | custom-call | flops 4000000000 | bytes 20000000 | tf_op jit(solution)/shard_map/local_part/pallas_call | solution.py:347
  23.1 0.0 copy-start.7
  23.1 0.8 copy-done.7
  23.9 0.0 copy-start.9
  23.9 0.8 copy-done.9
  24.7 5.9 %all-to-all-done = f32[64,1,1152]{2,1,0:T(1,128)S(1)} async-done(((f32[64,1,1152]{2,1,0:T(1,128)}), f32[64,1,1152]{2,1,0:T(1,128)S(1)}, u32[]{:S(2)}, u32[]{:S(2)}) %all-to-all-start) | async-done | bytes 294944 | tf_op jit(solution)/shard_map/all_to_all | solution.py:378
  30.6 0.2 scan_blocks.1
  30.7 18.5 %all_to_all.15 = f32[64,8,128]{2,1,0:T(8,128)S(1)} all-to-all(f32[64,8,128]{2,1,0:T(8,128)S(1)} %bitcast.7), channel_id=1, replica_groups=mesh['ctx'=64,'head'=16] {'ctx'}, dimensions={0} | all-to-all | bytes 524288 | tf_op jit(solution)/shard_map/all_to_all | solution.py:386
  49.2 1.4 %shared_grads.1 = f32[16,64,128]{2,1,0:T(8,128)} custom-call(f32[512,128]{1,0:T(8,128)S(1)} %bitcast.5, f32[512,128]{1,0:T(8,128)S(1)} %get-tuple-element.46.wl_ref, f32[512,128]{1,0:T(8,128)S(1)} %get-tuple-element.47.rl_ref, bf16[512,256]{1,0:T(8,128)(2,1)S(1)} %get-tuple-element.48.xh_ref, bf16[512,256]{1,0:T(8,128)(2,1)S(1)} %get-tuple-element.49.xl_ref, ...), custom_call_target="tpu_custom_call" | custom-call | flops 200000000 | bytes 2000000 | tf_op jit(solution)/shard_map/shared_grads/pallas_call | solution.py:347
  50.7 0.0 copy-start.8
  50.7 0.0 copy-start.10
  50.7 20.4 %all-to-all-start.2 = ((f32[16,64,128]{2,1,0:T(8,128)}), f32[16,64,128]{2,1,0:T(8,128)S(1)}, u32[]{:S(2)}, u32[]{:S(2)}) async-start(f32[16,64,128]{2,1,0:T(8,128)} %shared_grads.1), calls=%async_computation.2 | async-start | bytes 1048576 | tf_op jit(solution)/shard_map/all_to_all | solution.py:389
  71.0 0.0 copy-done.8
  71.0 0.0 copy-done.10
  71.0 4.0 %finish.1 = (bf16[512,256]{1,0:T(8,128)(2,1)}, bf16[512,256]{1,0:T(8,128)(2,1)}, f32[4,512]{1,0:T(4,128)}, f32[4,512]{1,0:T(4,128)}) custom-call(s32[4]{0:T(128)S(1)} %copy-done.6, f32[4,512]{1,0:T(4,128)S(1)} %copy-done.4, f32[4,512]{1,0:T(4,128)S(1)} %copy-done.5, bf16[512,128]{1,0:T(8,128)(2,1)S(1)} %copy-done.2, bf16[512,128]{1,0:T(8,128)(2,1)S(1)} %copy-done.3, ...), custom_call_target="tpu_custom_call" | custom-call | flops 4000000000 | bytes 20000000 | tf_op jit(solution)/shard_map/finish/pallas_call | solution.py:347
  75.1 13.3 %all-to-all-done.2.in_ref = f32[16,64,128]{2,1,0:T(8,128)S(1)} async-done(((f32[16,64,128]{2,1,0:T(8,128)}), f32[16,64,128]{2,1,0:T(8,128)S(1)}, u32[]{:S(2)}, u32[]{:S(2)}) %all-to-all-start.2) | async-done | bytes 524320 | tf_op jit(solution)/shard_map/all_to_all | solution.py:389
  88.4 0.6 add_heads.1
Async XLA Ops:
  0.6 17.3 %copy-start.2 = (bf16[512,128]{1,0:T(8,128)(2,1)S(1)}, bf16[512,128]{1,0:T(8,128)(2,1)}, u32[]{:S(2)}) copy-start(bf16[512,128]{1,0:T(8,128)(2,1)} %w_ref.1) | copy-start | bytes 393220
  0.6 17.3 %copy-start.3 = (bf16[512,128]{1,0:T(8,128)(2,1)S(1)}, bf16[512,128]{1,0:T(8,128)(2,1)}, u32[]{:S(2)}) copy-start(bf16[512,128]{1,0:T(8,128)(2,1)} %r_ref.1) | copy-start | bytes 393220
  3.6 14.3 %copy-start = (bf16[512,256]{1,0:T(8,128)(2,1)S(1)}, bf16[512,256]{1,0:T(8,128)(2,1)}, u32[]{:S(2)}) copy-start(bf16[512,256]{1,0:T(8,128)(2,1)} %x_ref.1) | copy-start | bytes 786436
  3.6 14.3 %copy-start.1 = (bf16[512,256]{1,0:T(8,128)(2,1)S(1)}, bf16[512,256]{1,0:T(8,128)(2,1)}, u32[]{:S(2)}) copy-start(bf16[512,256]{1,0:T(8,128)(2,1)} %g_ref.1) | copy-start | bytes 786436
  3.7 14.3 %copy-start.4 = (f32[4,512]{1,0:T(4,128)S(1)}, f32[4,512]{1,0:T(4,128)}, u32[]{:S(2)}) copy-start(f32[4,512]{1,0:T(4,128)} %ld_ref.1) | copy-start | bytes 24580
  3.7 14.3 %copy-start.5 = (f32[4,512]{1,0:T(4,128)S(1)}, f32[4,512]{1,0:T(4,128)}, u32[]{:S(2)}) copy-start(f32[4,512]{1,0:T(4,128)} %dt_ref.1) | copy-start | bytes 24580
  3.7 14.3 %copy-start.6 = (s32[4]{0:T(128)S(1)}, s32[4]{0:T(128)}, u32[]{:S(2)}) copy-start(s32[4]{0:T(128)} %len_ref.1) | copy-start | bytes 52
  3.7 26.9 %all-to-all-start = ((f32[64,1,1152]{2,1,0:T(1,128)}), f32[64,1,1152]{2,1,0:T(1,128)S(1)}, u32[]{:S(2)}, u32[]{:S(2)}) async-start(f32[64,1,1152]{2,1,0:T(1,128)} %bitcast.8), calls=%async_computation | async-start | bytes 589824 | tf_op jit(solution)/shard_map/all_to_all | solution.py:378
  23.1 0.8 copy-start.7
  23.9 0.8 copy-start.9
  50.7 20.4 %copy-start.8 = (f32[512,256]{1,0:T(8,128)S(1)}, f32[512,256]{1,0:T(8,128)}, u32[]{:S(2)}) copy-start(f32[512,256]{1,0:T(8,128)} %copy-done.7) | copy-start | bytes 1572868
  50.7 20.4 %copy-start.10 = (f32[512,256]{1,0:T(8,128)S(1)}, f32[512,256]{1,0:T(8,128)}, u32[]{:S(2)}) copy-start(f32[512,256]{1,0:T(8,128)} %copy-done.9) | copy-start | bytes 1572868
  50.7 37.7 %all-to-all-start.2 = ((f32[16,64,128]{2,1,0:T(8,128)}), f32[16,64,128]{2,1,0:T(8,128)S(1)}, u32[]{:S(2)}, u32[]{:S(2)}) async-start(f32[16,64,128]{2,1,0:T(8,128)} %shared_grads.1), calls=%async_computation.2 | async-start | bytes 1048576 | tf_op jit(solution)/shard_map/all_to_all | solution.py:389

commit v4 on v3

--- a/solution.py
+++ b/solution.py
@@ -1,3 +1,5 @@
+import functools
+
 import jax
 import jax.numpy as jnp
 from jax import lax
@@ -266,18 +268,25 @@
         wl_ref[rows, :] = wl
 
 
-def shared_grads(st_ref, wl_ref, rl_ref, xh_ref, xl_ref, gh_ref, gl_ref, out_ref):
-    steps = wl_ref.shape[0]
+def shared_grads(other, st_ref, wl_ref, rl_ref, xh_ref, xl_ref, gh_ref, gl_ref, out_ref):
+    groups, double, _ = out_ref.shape
+    share = double // 2
+    core = lax.rem(lax.axis_index("head"), 2)
+    core = 1 - core if other else core
     incoming, future = read_states(st_ref)
     s_hi, s_lo = split(incoming)
     f_hi, f_lo = split(future)
-    xh = xh_ref[...]
-    gh = gh_ref[...]
-    w = wl_ref[...] + mm(xh, f_hi, 1, 1) + mm(xh, f_lo, 1, 1) + mm(xl_ref[...], f_hi, 1, 1)
-    r = rl_ref[...] + mm(gh, s_hi, 1, 1) + mm(gh, s_lo, 1, 1) + mm(gl_ref[...], s_hi, 1, 1)
-    share = steps // out_ref.shape[0]
-    out_ref[:, 0:share, :] = w.reshape(out_ref.shape[0], share, w.shape[1])
-    out_ref[:, share:2 * share, :] = r.reshape(out_ref.shape[0], share, r.shape[1])
+
+    def mine(ref):
+        return jnp.concatenate([
+            ref[pl.ds(pl.multiple_of((2 * z + core) * share, share), share), :] for z in range(groups)], axis=0)
+
+    xh = mine(xh_ref)
+    gh = mine(gh_ref)
+    w = mine(wl_ref) + mm(xh, f_hi, 1, 1) + mm(xh, f_lo, 1, 1) + mm(mine(xl_ref), f_hi, 1, 1)
+    r = mine(rl_ref) + mm(gh, s_hi, 1, 1) + mm(gh, s_lo, 1, 1) + mm(mine(gl_ref), s_hi, 1, 1)
+    out_ref[:, 0:share, :] = w.reshape(groups, share, w.shape[1])
+    out_ref[:, share:double, :] = r.reshape(groups, share, r.shape[1])
 
 
 def finish(len_ref, ld_ref, dt_ref, w_ref, r_ref, x_ref, g_ref, y_ref, p_ref, st_ref,
@@ -384,9 +393,14 @@
     got, wl, rl = lax.optimization_barrier((got, wl, rl))
     scanned = call(scan_blocks, sds((blocks * 8, 128), F32), (got.reshape(blocks * PIECE, 128),), "scan_blocks", 1_000_000, 1_000_000)
     states = lax.all_to_all(scanned.reshape(blocks, 8, 128), "ctx", 0, 0).reshape(blocks * 8, 128)
-    terms = call(shared_grads, sds((groups, 2 * share, state), F32), (states, wl, rl, xh, xl, gh, gl),
-                 "shared_grads", 200_000_000, 2_000_000)
-    summed = lax.all_to_all(terms, "head", 0, 0)
+    parts = (states, wl, rl, xh, xl, gh, gl)
+    half = sds((groups // 2, 2 * share, state), F32)
+    theirs = call(functools.partial(shared_grads, True), half, parts, "shared_grads_other", 100_000_000, 1_000_000)
+    ours = call(functools.partial(shared_grads, False), half, parts, "shared_grads_own", 100_000_000, 1_000_000)
+    swapped = lax.ppermute(theirs, "head", [(i, i ^ 1) for i in range(groups)])
+    terms, y = lax.optimization_barrier((ours + swapped, y))
+    cores = [[2 * z + c for z in range(groups // 2)] for c in range(2)]
+    summed = lax.all_to_all(terms, "head", 0, 0, axis_index_groups=cores)
     outputs, input_grad, step_grad, decay_grad = call(
         finish,
         [sds((steps, width), BF16), sds((steps, width), BF16), sds((heads, steps), F32), sds((heads, steps), F32)],

time: 89.4 us -> 85.5 us (0.956)
  waiting for transfers between devices: 19.2 us -> 14.5 us
  starting transfers between devices: 34.6 us -> 36.8 us
    ppermute x0 -> x1, starting transfers between devices: none -> 8.33 us  [shards(): swapped = lax.ppermute(theirs, 'head', [(i, i ^ 1) for i in range(groups)])]
    all_to_all x1, waiting for transfers between devices: 13.3 us -> 7.06 us  [shards(): summed = lax.all_to_all(terms, 'head', 0, 0, axis_index_groups=cores)]
    all_to_all x1, starting transfers between devices: 20.4 us -> 14.3 us  [shards(): summed = lax.all_to_all(terms, 'head', 0, 0, axis_index_groups=cores)]
    pallas_call x6 -> x7, Pallas kernels: 14.3 us -> 13.7 us  [call(): pl.pallas_call(kernel, out_shape=outs, in_specs=[hbm if fetched else smem...]
  transfers between devices with their start and end apart: 2 -> 3, of which waited for: 2 -> 3; matrix products, arithmetic and copies ran while one was open for 0% -> 0% of each run, Pallas kernels for 10% -> 11%
where the time goes in v4:
time: 85.5 us; the launch traced here: 85.1 us
  starting transfers between devices  36.8 us (43%)
  blocking collectives  17.7 us (21%)
  waiting for transfers between devices  14.5 us (17%)
  Pallas kernels  13.7 us (16%)
    all_to_all x1, blocking collectives, shards(): lax.all_to_all(scanned.reshape(blocks, 8, 128), 'ctx', 0, 0)  17.7 us
    all_to_all x1, starting transfers between devices, shards(): summed = lax.all_to_all(terms, 'head', 0, 0, axis_index_groups=cores)  14.3 us
    all_to_all x1, starting transfers between devices, shards(): got = lax.all_to_all(pay.reshape(blocks, 1, PIECE * 128), 'ctx', 0, 0)  14.2 us
    pallas_call x7, Pallas kernels, call(): pl.pallas_call(kernel, out_shape=outs, in_specs=[hbm if fetched else smem...  13.7 us
    ppermute x1, starting transfers between devices, shards(): swapped = lax.ppermute(theirs, 'head', [(i, i ^ 1) for i in range(groups)])  8.33 us
    all_to_all x1, waiting for transfers between devices, shards(): summed = lax.all_to_all(terms, 'head', 0, 0, axis_index_groups=cores)  7.06 us
    all_to_all x1, waiting for transfers between devices, shards(): got = lax.all_to_all(pay.reshape(blocks, 1, PIECE * 128), 'ctx', 0, 0)  6.71 us
  transfers between devices with their start and end apart: 3, of which 3 were waited for; matrix products, arithmetic and copies ran while one was open for 0% of the time, Pallas kernels for 11%

profile of v4, /device:TPU:1, one launch (start us, length us, event | category | flops | bytes accessed | tf_op | source)
XLA Modules:
  0.0 85.1 jit_solution(4497507193632243410)
XLA Ops:
  0.6 0.0 copy-start.2
  0.6 0.0 copy-start.3
  0.7 3.0 %state_terms.1 = f32[576,128]{1,0:T(8,128)} custom-call(s32[4]{0:T(128)} %len_ref.1, f32[4,512]{1,0:T(4,128)} %ld_ref.1, f32[4,512]{1,0:T(4,128)} %dt_ref.1, bf16[512,128]{1,0:T(8,128)(2,1)} %w_ref.1, bf16[512,128]{1,0:T(8,128)(2,1)} %r_ref.1, bf16[512,256]{1,0:T(8,128)(2,1)} %x_ref.1, bf16[512,256]{1,0:T(8,128)(2,1)} %g_ref.1), custom_call_target="tpu_custom_call" | custom-call | flops 200000000 | bytes 2000000 | tf_op jit(solution)/shard_map/state_terms/pallas_call | solution.py:356
  3.6 0.0 copy-start
  3.7 0.0 copy-start.1
  3.7 0.0 copy-start.4
  3.7 0.0 copy-start.5
  3.7 0.0 copy-start.6
  3.7 14.2 %all-to-all-start = ((f32[64,1,1152]{2,1,0:T(1,128)}), f32[64,1,1152]{2,1,0:T(1,128)S(1)}, u32[]{:S(2)}, u32[]{:S(2)}) async-start(f32[64,1,1152]{2,1,0:T(1,128)} %bitcast.9), calls=%async_computation | async-start | bytes 589824 | tf_op jit(solution)/shard_map/all_to_all | solution.py:387
  17.9 0.0 copy-done.2
  17.9 0.0 copy-done.3
  17.9 0.0 copy-done
  17.9 0.0 copy-done.1
  17.9 0.0 copy-done.4
  17.9 0.0 copy-done.5
  18.0 0.0 copy-done.6
  18.0 5.1 %local_part.1 = (f32[512,256]{1,0:T(8,128)S(1)}, f32[512,256]{1,0:T(8,128)S(1)}, f32[512,128]{1,0:T(8,128)S(1)}, f32[512,128]{1,0:T(8,128)S(1)}, bf16[512,256]{1...) custom-call(s32[4]{0:T(128)S(1)} %copy-done.6, ...), custom_call_target="tpu_custom_call" | custom-call | flops 4000000000 | bytes 20000000 | tf_op jit(solution)/shard_map/local_part/pallas_call | solution.py:356
  23.1 0.0 copy-start.7
  23.1 0.8 copy-done.7
  23.9 6.7 %all-to-all-done = f32[64,1,1152]{2,1,0:T(1,128)S(1)} async-done(((f32[64,1,1152]{2,1,0:T(1,128)}), f32[64,1,1152]{2,1,0:T(1,128)S(1)}, u32[]{:S(2)}, u32[]{:S(2)}) %all-to-all-start) | async-done | bytes 294944 | tf_op jit(solution)/shard_map/all_to_all | solution.py:387
  30.6 0.2 scan_blocks.1
  30.8 17.7 %all_to_all.15 = f32[64,8,128]{2,1,0:T(8,128)S(1)} all-to-all(f32[64,8,128]{2,1,0:T(8,128)S(1)} %bitcast.8), channel_id=1, replica_groups=mesh['ctx'=64,'head'=16] {'ctx'}, dimensions={0} | all-to-all | bytes 524288 | tf_op jit(solution)/shard_map/all_to_all | solution.py:395
  48.4 0.4 shared_grads_other.1
  48.8 8.3 %collective-permute-start = (f32[8,64,128]{2,1,0:T(8,128)S(1)}, f32[8,64,128]{2,1,0:T(8,128)S(1)}, u32[]{:S(2)}, u32[]{:S(2)}) collective-permute-start(f32[8,64,128]{2,1,0:T(8,128)S(1)} %shared_grads_other.1), channel_id=1, source_target_pairs={{0,1},{1,0},{2,3},{3,2},{4,5},{5,4},{6,7},{7,6},{8,9},{9,8},{10,11... | collective-permute-start | bytes 786440 | tf_op jit(solution)/shard_map/ppermute | solution.py:400
  57.2 0.4 shared_grads_own.1
  57.6 0.0 copy-start.8
  57.6 0.7 collective-permute-done
  58.3 0.7 add.3
  59.0 14.3 %all-to-all-start.2 = ((f32[8,64,128]{2,1,0:T(8,128)}), f32[8,64,128]{2,1,0:T(8,128)S(1)}, u32[]{:S(2)}, u32[]{:S(2)}) async-start(f32[8,64,128]{2,1,0:T(8,128)} %add.3), calls=%async_computation.2 | async-start | bytes 524288 | tf_op jit(solution)/shard_map/all_to_all | solution.py:403
  73.4 0.0 copy-done.8
  73.4 4.0 %finish.1 = (bf16[512,256]{1,0:T(8,128)(2,1)}, bf16[512,256]{1,0:T(8,128)(2,1)}, f32[4,512]{1,0:T(4,128)}, f32[4,512]{1,0:T(4,128)}) custom-call(s32[4]{0:T(128)S(1)} %copy-done.6, f32[4,512]{1,0:T(4,128)S(1)} %copy-done.4, f32[4,512]{1,0:T(4,128)S(1)} %copy-done.5, bf16[512,128]{1,0:T(8,128)(2,1)S(1)} %copy-done.2, bf16[512,128]{1,0:T(8,128)(2,1)S(1)} %copy-done.3, ...), custom_call_target="tpu_custom_call" | custom-call | flops 4000000000 | bytes 20000000 | tf_op jit(solution)/shard_map/finish/pallas_call | solution.py:356
  77.4 7.1 %all-to-all-done.2.in_ref = f32[8,64,128]{2,1,0:T(8,128)S(1)} async-done(((f32[8,64,128]{2,1,0:T(8,128)}), f32[8,64,128]{2,1,0:T(8,128)S(1)}, u32[]{:S(2)}, u32[]{:S(2)}) %all-to-all-start.2) | async-done | bytes 262176 | tf_op jit(solution)/shard_map/all_to_all | solution.py:403
  84.5 0.6 add_heads.1
Async XLA Ops:
  0.6 17.3 %copy-start.2 = (bf16[512,128]{1,0:T(8,128)(2,1)S(1)}, bf16[512,128]{1,0:T(8,128)(2,1)}, u32[]{:S(2)}) copy-start(bf16[512,128]{1,0:T(8,128)(2,1)} %w_ref.1) | copy-start | bytes 393220
  0.6 17.3 %copy-start.3 = (bf16[512,128]{1,0:T(8,128)(2,1)S(1)}, bf16[512,128]{1,0:T(8,128)(2,1)}, u32[]{:S(2)}) copy-start(bf16[512,128]{1,0:T(8,128)(2,1)} %r_ref.1) | copy-start | bytes 393220
  3.6 14.3 %copy-start = (bf16[512,256]{1,0:T(8,128)(2,1)S(1)}, bf16[512,256]{1,0:T(8,128)(2,1)}, u32[]{:S(2)}) copy-start(bf16[512,256]{1,0:T(8,128)(2,1)} %x_ref.1) | copy-start | bytes 786436
  3.7 14.3 %copy-start.1 = (bf16[512,256]{1,0:T(8,128)(2,1)S(1)}, bf16[512,256]{1,0:T(8,128)(2,1)}, u32[]{:S(2)}) copy-start(bf16[512,256]{1,0:T(8,128)(2,1)} %g_ref.1) | copy-start | bytes 786436
  3.7 14.3 %copy-start.4 = (f32[4,512]{1,0:T(4,128)S(1)}, f32[4,512]{1,0:T(4,128)}, u32[]{:S(2)}) copy-start(f32[4,512]{1,0:T(4,128)} %ld_ref.1) | copy-start | bytes 24580
  3.7 14.3 %copy-start.5 = (f32[4,512]{1,0:T(4,128)S(1)}, f32[4,512]{1,0:T(4,128)}, u32[]{:S(2)}) copy-start(f32[4,512]{1,0:T(4,128)} %dt_ref.1) | copy-start | bytes 24580
  3.7 14.3 %copy-start.6 = (s32[4]{0:T(128)S(1)}, s32[4]{0:T(128)}, u32[]{:S(2)}) copy-start(s32[4]{0:T(128)} %len_ref.1) | copy-start | bytes 52
  3.7 26.9 %all-to-all-start = ((f32[64,1,1152]{2,1,0:T(1,128)}), f32[64,1,1152]{2,1,0:T(1,128)S(1)}, u32[]{:S(2)}, u32[]{:S(2)}) async-start(f32[64,1,1152]{2,1,0:T(1,128)} %bitcast.9), calls=%async_computation | async-start | bytes 589824 | tf_op jit(solution)/shard_map/all_to_all | solution.py:387
  23.1 0.8 copy-start.7
  48.8 9.5 %collective-permute-start = (f32[8,64,128]{2,1,0:T(8,128)S(1)}, f32[8,64,128]{2,1,0:T(8,128)S(1)}, u32[]{:S(2)}, u32[]{:S(2)}) collective-permute-start(f32[8,64,128]{2,1,0:T(8,128)S(1)} %shared_grads_other.1), channel_id=1, source_target_pairs={{0,1},{1,0},{2,3},{3,2},{4,5},{5,4},{6,7},{7,6},{8,9},{9,8},{10,11... | collective-permute-start | bytes 786440 | tf_op jit(solution)/shard_map/ppermute | solution.py:400
  57.6 15.8 %copy-start.8 = (f32[512,256]{1,0:T(8,128)S(1)}, f32[512,256]{1,0:T(8,128)}, u32[]{:S(2)}) copy-start(f32[512,256]{1,0:T(8,128)} %copy-done.7) | copy-start | bytes 1572868
  59.0 25.4 %all-to-all-start.2 = ((f32[8,64,128]{2,1,0:T(8,128)}), f32[8,64,128]{2,1,0:T(8,128)S(1)}, u32[]{:S(2)}, u32[]{:S(2)}) async-start(f32[8,64,128]{2,1,0:T(8,128)} %add.3), calls=%async_computation.2 | async-start | bytes 524288 | tf_op jit(solution)/shard_map/all_to_all | solution.py:403

commit v5 on v4

--- a/solution.py
+++ b/solution.py
@@ -125,10 +125,10 @@
     for half in range(2):
         lanes = slice(128 * half, 128 * half + 128)
         base = half_rows * half
-        x_hi, x_lo = scaled(x_ref, lanes, 2 * half)
-        fresh = mm(w, x_hi, 0, 0) + mm(w, x_lo, 0, 0)
-        g_hi, g_lo = scaled(g_ref, lanes, heads + 2 * half)
-        back = mm(r, g_hi, 0, 0) + mm(r, g_lo, 0, 0)
+        both = mm(w, jnp.concatenate(scaled(x_ref, lanes, 2 * half), axis=1), 0, 0)
+        fresh = both[:, 0:128] + both[:, 128:256]
+        both = mm(r, jnp.concatenate(scaled(g_ref, lanes, heads + 2 * half), axis=1), 0, 0)
+        back = both[:, 0:128] + both[:, 128:256]
         for i in range(4):
             rows = slice(32 * i, 32 * i + 32)
             pay_ref[pl.ds(base + i, 32, stride=PIECE), :] = fresh[rows]
@@ -213,8 +213,9 @@
         gc = split(gf * enter_lanes)
         w = w_ref[rows, :]
         r = r_ref[rows, :]
-        fresh = mm(w, xc[0], 0, 0) + mm(w, xc[1], 0, 0)
-        back = mm(r, gc[0], 0, 0) + mm(r, gc[1], 0, 0)
+        two = lambda m: jnp.concatenate([m, m], axis=0)
+        fresh = mm(two(w), jnp.concatenate(xc, axis=0), 0, 0)
+        back = mm(two(r), jnp.concatenate(gc, axis=0), 0, 0)
         keep_row = jnp.concatenate([
             jnp.where(iota((1, 128), 1) < 64, keep[h:h + 1, :], keep[h + 1:h + 2, :])
             for h in range(0, heads, 2)], axis=1)
@@ -222,32 +223,38 @@
         scores = mm(r, w, 1, 1)
         total_e = jnp.zeros((CHUNK, CHUNK), F32)
         y_parts, p_parts = [], []
-        for h in range(heads):
-            pair = slice(128 * (h // 2), 128 * (h // 2) + 128)
+        for first_head in range(0, heads, 2):
+            pair = slice(64 * first_head, 64 * first_head + 128)
             x_pair = x[:, pair]
             g_pair = g[:, pair]
-            mine = low if h % 2 == 0 else ~low
-            decays = jnp.exp(jnp.where(inside, cols[:, h:h + 1] - cum[h:h + 1, :], NEG))
-            weighted = scores * decays
-            dt_row = dt[h:h + 1, :]
-            a_hi, a_lo = split(weighted * dt_row)
-            y_parts.append(mm(a_hi, x_pair, 1, 0) + mm(a_lo, x_pair, 1, 0))
-            b_hi, b_lo = split(weighted)
-            p_parts.append(mm(b_hi, g_pair, 0, 0) + mm(b_lo, g_pair, 0, 0))
-            g_mine = jnp.where(mine, gf[:, pair], 0.0).astype(BF16)
-            total_e = total_e + decays * dt_row * mm(g_mine, x_pair, 1, 1)
-        y = jnp.concatenate([jnp.where(low, y_parts[h], y_parts[h + 1]) for h in range(0, heads, 2)], axis=1)
-        p = jnp.concatenate([jnp.where(low, p_parts[h], p_parts[h + 1]) for h in range(0, heads, 2)], axis=1)
+            g_both = jnp.concatenate([
+                jnp.where(low, gf[:, pair], 0.0).astype(BF16), jnp.where(low, 0.0, gf[:, pair]).astype(BF16)], axis=0)
+            dots = mm(g_both, x_pair, 1, 1)
+            forward, backward = [], []
+            for k in range(2):
+                h = first_head + k
+                decays = jnp.exp(jnp.where(inside, cols[:, h:h + 1] - cum[h:h + 1, :], NEG))
+                weighted = scores * decays
+                dt_row = dt[h:h + 1, :]
+                forward.append(jnp.concatenate(split(weighted * dt_row), axis=1))
+                backward.append(jnp.concatenate(split(weighted), axis=0))
+                total_e = total_e + decays * dt_row * dots[k * CHUNK:(k + 1) * CHUNK, :]
+            y2 = mm(jnp.concatenate(forward, axis=0), jnp.concatenate([x_pair, x_pair], axis=0), 1, 0)
+            p2 = mm(jnp.concatenate(backward, axis=1), jnp.concatenate([g_pair, g_pair], axis=0), 0, 0)
+            y_parts.append(jnp.where(low, y2[0:CHUNK], y2[CHUNK:2 * CHUNK]))
+            p_parts.append(jnp.where(low, p2[0:CHUNK], p2[CHUNK:2 * CHUNK]))
+        y = jnp.concatenate(y_parts, axis=1)
+        p = jnp.concatenate(p_parts, axis=1)
         e_hi, e_lo = split(total_e)
-        wl = mm(e_hi, r, 0, 0) + mm(e_lo, r, 0, 0)
-        rl = mm(e_hi, w, 1, 0) + mm(e_lo, w, 1, 0)
+        wl = mm(jnp.concatenate([e_hi, e_lo], axis=0), two(r), 0, 0)
+        rl = mm(jnp.concatenate([e_hi, e_lo], axis=1), two(w), 1, 0)
         saved.append((rows, y, p, wl, rl, xc, gc, w, r, fresh, back, keep_row, enter_lanes, leave_lanes))
     state = None
     for q in range(chunks):
         rows, y, p, wl, rl, xc, gc, w, r, fresh, back, keep_row, enter_lanes, leave_lanes = saved[q]
         if state is not None:
             s_hi, s_lo = split(state)
-            y = y + enter_lanes * (mm(r, s_hi, 1, 0) + mm(r, s_lo, 1, 0))
+            y = y + enter_lanes * mm(jnp.concatenate([r, r], axis=1), jnp.concatenate([s_hi, s_lo], axis=0), 1, 0)
             rl = rl + (mm(gc[0], s_hi, 1, 1) + mm(gc[0], s_lo, 1, 1) + mm(gc[1], s_hi, 1, 1))
             state = state * keep_row + fresh
         else:
@@ -259,7 +266,7 @@
         rows, y, p, wl, rl, xc, gc, w, r, fresh, back, keep_row, enter_lanes, leave_lanes = saved[q]
         if future is not None:
             f_hi, f_lo = split(future)
-            p = p + leave_lanes * (mm(w, f_hi, 1, 0) + mm(w, f_lo, 1, 0))
+            p = p + leave_lanes * mm(jnp.concatenate([w, w], axis=1), jnp.concatenate([f_hi, f_lo], axis=0), 1, 0)
             wl = wl + (mm(xc[0], f_hi, 1, 1) + mm(xc[0], f_lo, 1, 1) + mm(xc[1], f_hi, 1, 1))
             future = future * keep_row + back
         else:

time: 85.5 us -> 85.4 us (level)
  transfers between devices with their start and end apart: 3 -> 3, of which waited for: 3 -> 3; matrix products, arithmetic and copies ran while one was open for 0% -> 0% of each run, Pallas kernels for 11% -> 10%
where the time goes in v5:
time: 85.4 us; the launch traced here: 85 us
  starting transfers between devices  37.6 us (44%)
  blocking collectives  17 us (20%)
  waiting for transfers between devices  15.2 us (18%)
  Pallas kernels  12.9 us (15%)
    all_to_all x1, blocking collectives, shards(): lax.all_to_all(scanned.reshape(blocks, 8, 128), 'ctx', 0, 0)  17 us
    all_to_all x1, starting transfers between devices, shards(): summed = lax.all_to_all(terms, 'head', 0, 0, axis_index_groups=cores)  15.1 us
    all_to_all x1, starting transfers between devices, shards(): got = lax.all_to_all(pay.reshape(blocks, 1, PIECE * 128), 'ctx', 0, 0)  14.2 us
    pallas_call x7, Pallas kernels, call(): pl.pallas_call(kernel, out_shape=outs, in_specs=[hbm if fetched else smem...  12.9 us
    ppermute x1, starting transfers between devices, shards(): swapped = lax.ppermute(theirs, 'head', [(i, i ^ 1) for i in range(groups)])  8.34 us
    all_to_all x1, waiting for transfers between devices, shards(): got = lax.all_to_all(pay.reshape(blocks, 1, PIECE * 128), 'ctx', 0, 0)  7.43 us
    all_to_all x1, waiting for transfers between devices, shards(): summed = lax.all_to_all(terms, 'head', 0, 0, axis_index_groups=cores)  7.06 us
  transfers between devices with their start and end apart: 3, of which 3 were waited for; matrix products, arithmetic and copies ran while one was open for 0% of the time, Pallas kernels for 10%

profile of v5, /device:TPU:1, one launch (start us, length us, event | category | flops | bytes accessed | tf_op | source)
XLA Modules:
  0.0 85.0 jit_solution(7104605884460249443)
XLA Ops:
  0.6 0.0 copy-start.2
  0.6 0.0 copy-start.3
  0.7 2.9 %state_terms.1 = f32[576,128]{1,0:T(8,128)} custom-call(s32[4]{0:T(128)} %len_ref.1, f32[4,512]{1,0:T(4,128)} %ld_ref.1, f32[4,512]{1,0:T(4,128)} %dt_ref.1, bf16[512,128]{1,0:T(8,128)(2,1)} %w_ref.1, bf16[512,128]{1,0:T(8,128)(2,1)} %r_ref.1, bf16[512,256]{1,0:T(8,128)(2,1)} %x_ref.1, bf16[512,256]{1,0:T(8,128)(2,1)} %g_ref.1), custom_call_target="tpu_custom_call" | custom-call | flops 200000000 | bytes 2000000 | tf_op jit(solution)/shard_map/state_terms/pallas_call | solution.py:363
  3.6 0.0 copy-start
  3.6 0.0 copy-start.1
  3.6 0.0 copy-start.4
  3.6 0.0 copy-start.5
  3.6 0.0 copy-start.6
  3.7 14.2 %all-to-all-start = ((f32[64,1,1152]{2,1,0:T(1,128)}), f32[64,1,1152]{2,1,0:T(1,128)S(1)}, u32[]{:S(2)}, u32[]{:S(2)}) async-start(f32[64,1,1152]{2,1,0:T(1,128)} %bitcast.9), calls=%async_computation | async-start | bytes 589824 | tf_op jit(solution)/shard_map/all_to_all | solution.py:394
  17.8 0.0 copy-done.2
  17.8 0.0 copy-done.3
  17.9 0.0 copy-done
  17.9 0.0 copy-done.1
  17.9 0.0 copy-done.4
  17.9 0.0 copy-done.5
  17.9 0.0 copy-done.6
  17.9 4.4 %local_part.1 = (f32[512,256]{1,0:T(8,128)S(1)}, f32[512,256]{1,0:T(8,128)S(1)}, f32[512,128]{1,0:T(8,128)S(1)}, f32[512,128]{1,0:T(8,128)S(1)}, bf16[512,256]{1...) custom-call(s32[4]{0:T(128)S(1)} %copy-done.6, ...), custom_call_target="tpu_custom_call" | custom-call | flops 4000000000 | bytes 20000000 | tf_op jit(solution)/shard_map/local_part/pallas_call | solution.py:363
  22.3 0.0 copy-start.7
  22.3 0.8 copy-done.7
  23.1 7.4 %all-to-all-done = f32[64,1,1152]{2,1,0:T(1,128)S(1)} async-done(((f32[64,1,1152]{2,1,0:T(1,128)}), f32[64,1,1152]{2,1,0:T(1,128)S(1)}, u32[]{:S(2)}, u32[]{:S(2)}) %all-to-all-start) | async-done | bytes 294944 | tf_op jit(solution)/shard_map/all_to_all | solution.py:394
  30.5 0.2 scan_blocks.1
  30.7 17.0 %all_to_all.15 = f32[64,8,128]{2,1,0:T(8,128)S(1)} all-to-all(f32[64,8,128]{2,1,0:T(8,128)S(1)} %bitcast.8), channel_id=1, replica_groups=mesh['ctx'=64,'head'=16] {'ctx'}, dimensions={0} | all-to-all | bytes 524288 | tf_op jit(solution)/shard_map/all_to_all | solution.py:402
  47.7 0.4 shared_grads_other.1
  48.0 8.3 %collective-permute-start = (f32[8,64,128]{2,1,0:T(8,128)S(1)}, f32[8,64,128]{2,1,0:T(8,128)S(1)}, u32[]{:S(2)}, u32[]{:S(2)}) collective-permute-start(f32[8,64,128]{2,1,0:T(8,128)S(1)} %shared_grads_other.1), channel_id=1, source_target_pairs={{0,1},{1,0},{2,3},{3,2},{4,5},{5,4},{6,7},{7,6},{8,9},{9,8},{10,11... | collective-permute-start | bytes 786440 | tf_op jit(solution)/shard_map/ppermute | solution.py:407
  56.4 0.4 shared_grads_own.1
  56.8 0.0 copy-start.8
  56.8 0.7 collective-permute-done
  57.5 0.7 add.3
  58.3 15.1 %all-to-all-start.2 = ((f32[8,64,128]{2,1,0:T(8,128)}), f32[8,64,128]{2,1,0:T(8,128)S(1)}, u32[]{:S(2)}, u32[]{:S(2)}) async-start(f32[8,64,128]{2,1,0:T(8,128)} %add.3), calls=%async_computation.2 | async-start | bytes 524288 | tf_op jit(solution)/shard_map/all_to_all | solution.py:410
  73.3 0.0 copy-done.8
  73.3 4.0 %finish.1 = (bf16[512,256]{1,0:T(8,128)(2,1)}, bf16[512,256]{1,0:T(8,128)(2,1)}, f32[4,512]{1,0:T(4,128)}, f32[4,512]{1,0:T(4,128)}) custom-call(s32[4]{0:T(128)S(1)} %copy-done.6, f32[4,512]{1,0:T(4,128)S(1)} %copy-done.4, f32[4,512]{1,0:T(4,128)S(1)} %copy-done.5, bf16[512,128]{1,0:T(8,128)(2,1)S(1)} %copy-done.2, bf16[512,128]{1,0:T(8,128)(2,1)S(1)} %copy-done.3, ...), custom_call_target="tpu_custom_call" | custom-call | flops 4000000000 | bytes 20000000 | tf_op jit(solution)/shard_map/finish/pallas_call | solution.py:363
  77.4 7.1 %all-to-all-done.2.in_ref = f32[8,64,128]{2,1,0:T(8,128)S(1)} async-done(((f32[8,64,128]{2,1,0:T(8,128)}), f32[8,64,128]{2,1,0:T(8,128)S(1)}, u32[]{:S(2)}, u32[]{:S(2)}) %all-to-all-start.2) | async-done | bytes 262176 | tf_op jit(solution)/shard_map/all_to_all | solution.py:410
  84.4 0.6 add_heads.1
Async XLA Ops:
  0.6 17.2 %copy-start.2 = (bf16[512,128]{1,0:T(8,128)(2,1)S(1)}, bf16[512,128]{1,0:T(8,128)(2,1)}, u32[]{:S(2)}) copy-start(bf16[512,128]{1,0:T(8,128)(2,1)} %w_ref.1) | copy-start | bytes 393220
  0.6 17.2 %copy-start.3 = (bf16[512,128]{1,0:T(8,128)(2,1)S(1)}, bf16[512,128]{1,0:T(8,128)(2,1)}, u32[]{:S(2)}) copy-start(bf16[512,128]{1,0:T(8,128)(2,1)} %r_ref.1) | copy-start | bytes 393220
  3.6 14.3 %copy-start = (bf16[512,256]{1,0:T(8,128)(2,1)S(1)}, bf16[512,256]{1,0:T(8,128)(2,1)}, u32[]{:S(2)}) copy-start(bf16[512,256]{1,0:T(8,128)(2,1)} %x_ref.1) | copy-start | bytes 786436
  3.6 14.3 %copy-start.1 = (bf16[512,256]{1,0:T(8,128)(2,1)S(1)}, bf16[512,256]{1,0:T(8,128)(2,1)}, u32[]{:S(2)}) copy-start(bf16[512,256]{1,0:T(8,128)(2,1)} %g_ref.1) | copy-start | bytes 786436
  3.6 14.3 %copy-start.4 = (f32[4,512]{1,0:T(4,128)S(1)}, f32[4,512]{1,0:T(4,128)}, u32[]{:S(2)}) copy-start(f32[4,512]{1,0:T(4,128)} %ld_ref.1) | copy-start | bytes 24580
  3.6 14.3 %copy-start.5 = (f32[4,512]{1,0:T(4,128)S(1)}, f32[4,512]{1,0:T(4,128)}, u32[]{:S(2)}) copy-start(f32[4,512]{1,0:T(4,128)} %dt_ref.1) | copy-start | bytes 24580
  3.6 14.3 %copy-start.6 = (s32[4]{0:T(128)S(1)}, s32[4]{0:T(128)}, u32[]{:S(2)}) copy-start(s32[4]{0:T(128)} %len_ref.1) | copy-start | bytes 52
  3.7 26.9 %all-to-all-start = ((f32[64,1,1152]{2,1,0:T(1,128)}), f32[64,1,1152]{2,1,0:T(1,128)S(1)}, u32[]{:S(2)}, u32[]{:S(2)}) async-start(f32[64,1,1152]{2,1,0:T(1,128)} %bitcast.9), calls=%async_computation | async-start | bytes 589824 | tf_op jit(solution)/shard_map/all_to_all | solution.py:394
  22.3 0.8 copy-start.7
  48.0 9.5 %collective-permute-start = (f32[8,64,128]{2,1,0:T(8,128)S(1)}, f32[8,64,128]{2,1,0:T(8,128)S(1)}, u32[]{:S(2)}, u32[]{:S(2)}) collective-permute-start(f32[8,64,128]{2,1,0:T(8,128)S(1)} %shared_grads_other.1), channel_id=1, source_target_pairs={{0,1},{1,0},{2,3},{3,2},{4,5},{5,4},{6,7},{7,6},{8,9},{9,8},{10,11... | collective-permute-start | bytes 786440 | tf_op jit(solution)/shard_map/ppermute | solution.py:407
  56.8 16.5 %copy-start.8 = (f32[512,256]{1,0:T(8,128)S(1)}, f32[512,256]{1,0:T(8,128)}, u32[]{:S(2)}) copy-start(f32[512,256]{1,0:T(8,128)} %copy-done.7) | copy-start | bytes 1572868
  58.3 26.1 %all-to-all-start.2 = ((f32[8,64,128]{2,1,0:T(8,128)}), f32[8,64,128]{2,1,0:T(8,128)S(1)}, u32[]{:S(2)}, u32[]{:S(2)}) async-start(f32[8,64,128]{2,1,0:T(8,128)} %add.3), calls=%async_computation.2 | async-start | bytes 524288 | tf_op jit(solution)/shard_map/all_to_all | solution.py:410

commit v6 on v5

--- a/solution.py
+++ b/solution.py
@@ -412,8 +412,8 @@
         finish,
         [sds((steps, width), BF16), sds((steps, width), BF16), sds((heads, steps), F32), sds((heads, steps), F32)],
         common + (y, p, states), "finish", 4_000_000_000, 20_000_000)
-    write_grad, read_grad = call(
-        add_heads, [sds((share, state), F32), sds((share, state), F32)], (summed,), "add_heads", 1_000_000, 1_000_000)
+    total = jnp.sum(summed, axis=0)
+    write_grad, read_grad = total[0:share], total[share:2 * share]
     return (outputs, input_grad, write_grad, read_grad, step_grad, decay_grad)
 
 

time: 85.4 us -> 85.4 us (level)
    pallas_call x7 -> x6, Pallas kernels: 12.9 us -> 12.3 us  [call(): pl.pallas_call(kernel, out_shape=outs, in_specs=[hbm if fetched else smem...]
where the time goes in v6:
time: 85.4 us; the launch traced here: 85.1 us
  starting transfers between devices  37.6 us (44%)
  blocking collectives  17 us (20%)
  waiting for transfers between devices  15.2 us (18%)
  Pallas kernels  12.3 us (14%)
  local copies, waits for them, and re-layouts  1.44 us (2%)
    all_to_all x1, blocking collectives, shards(): lax.all_to_all(scanned.reshape(blocks, 8, 128), 'ctx', 0, 0)  17 us
    all_to_all x1, starting transfers between devices, shards(): summed = lax.all_to_all(terms, 'head', 0, 0, axis_index_groups=cores)  15.1 us
    all_to_all x1, starting transfers between devices, shards(): got = lax.all_to_all(pay.reshape(blocks, 1, PIECE * 128), 'ctx', 0, 0)  14.2 us
    pallas_call x6, Pallas kernels, call(): pl.pallas_call(kernel, out_shape=outs, in_specs=[hbm if fetched else smem...  12.3 us
    ppermute x1, starting transfers between devices, shards(): swapped = lax.ppermute(theirs, 'head', [(i, i ^ 1) for i in range(groups)])  8.33 us
    all_to_all x1, waiting for transfers between devices, shards(): got = lax.all_to_all(pay.reshape(blocks, 1, PIECE * 128), 'ctx', 0, 0)  7.43 us
    all_to_all x1, waiting for transfers between devices, shards(): summed = lax.all_to_all(terms, 'head', 0, 0, axis_index_groups=cores)  7.06 us
  transfers between devices with their start and end apart: 3, of which 3 were waited for; matrix products, arithmetic and copies ran while one was open for 0% of the time, Pallas kernels for 10%

profile of v6, /device:TPU:1, one launch (start us, length us, event | category | flops | bytes accessed | tf_op | source)
XLA Modules:
  0.0 85.1 jit_solution(14883406818301171211)
XLA Ops:
  0.6 0.0 copy-start.2
  0.6 0.0 copy-start.3
  0.7 2.9 %state_terms.1 = f32[576,128]{1,0:T(8,128)} custom-call(s32[4]{0:T(128)} %len_ref.1, f32[4,512]{1,0:T(4,128)} %ld_ref.1, f32[4,512]{1,0:T(4,128)} %dt_ref.1, bf16[512,128]{1,0:T(8,128)(2,1)} %w_ref.1, bf16[512,128]{1,0:T(8,128)(2,1)} %r_ref.1, bf16[512,256]{1,0:T(8,128)(2,1)} %x_ref.1, bf16[512,256]{1,0:T(8,128)(2,1)} %g_ref.1), custom_call_target="tpu_custom_call" | custom-call | flops 200000000 | bytes 2000000 | tf_op jit(solution)/shard_map/state_terms/pallas_call | solution.py:363
  3.6 0.0 copy-start
  3.6 0.0 copy-start.1
  3.6 0.0 copy-start.4
  3.6 0.0 copy-start.5
  3.6 0.0 copy-start.6
  3.6 14.2 %all-to-all-start = ((f32[64,1,1152]{2,1,0:T(1,128)}), f32[64,1,1152]{2,1,0:T(1,128)S(1)}, u32[]{:S(2)}, u32[]{:S(2)}) async-start(f32[64,1,1152]{2,1,0:T(1,128)} %bitcast.9), calls=%async_computation | async-start | bytes 589824 | tf_op jit(solution)/shard_map/all_to_all | solution.py:394
  17.8 0.0 copy-done.2
  17.8 0.0 copy-done.3
  17.9 0.0 copy-done
  17.9 0.0 copy-done.1
  17.9 0.0 copy-done.4
  17.9 0.0 copy-done.5
  17.9 0.0 copy-done.6
  17.9 4.4 %local_part.1 = (f32[512,256]{1,0:T(8,128)S(1)}, f32[512,256]{1,0:T(8,128)S(1)}, f32[512,128]{1,0:T(8,128)S(1)}, f32[512,128]{1,0:T(8,128)S(1)}, bf16[512,256]{1...) custom-call(s32[4]{0:T(128)S(1)} %copy-done.6, ...), custom_call_target="tpu_custom_call" | custom-call | flops 4000000000 | bytes 20000000 | tf_op jit(solution)/shard_map/local_part/pallas_call | solution.py:363
  22.3 0.0 copy-start.7
  22.3 0.8 copy-done.7
  23.1 7.4 %all-to-all-done = f32[64,1,1152]{2,1,0:T(1,128)S(1)} async-done(((f32[64,1,1152]{2,1,0:T(1,128)}), f32[64,1,1152]{2,1,0:T(1,128)S(1)}, u32[]{:S(2)}, u32[]{:S(2)}) %all-to-all-start) | async-done | bytes 294944 | tf_op jit(solution)/shard_map/all_to_all | solution.py:394
  30.5 0.2 scan_blocks.1
  30.7 17.0 %all_to_all.15 = f32[64,8,128]{2,1,0:T(8,128)S(1)} all-to-all(f32[64,8,128]{2,1,0:T(8,128)S(1)} %bitcast.8), channel_id=1, replica_groups=mesh['ctx'=64,'head'=16] {'ctx'}, dimensions={0} | all-to-all | bytes 524288 | tf_op jit(solution)/shard_map/all_to_all | solution.py:402
  47.7 0.4 shared_grads_other.1
  48.0 8.3 %collective-permute-start = (f32[8,64,128]{2,1,0:T(8,128)S(1)}, f32[8,64,128]{2,1,0:T(8,128)S(1)}, u32[]{:S(2)}, u32[]{:S(2)}) collective-permute-start(f32[8,64,128]{2,1,0:T(8,128)S(1)} %shared_grads_other.1), channel_id=1, source_target_pairs={{0,1},{1,0},{2,3},{3,2},{4,5},{5,4},{6,7},{7,6},{8,9},{9,8},{10,11... | collective-permute-start | bytes 786440 | tf_op jit(solution)/shard_map/ppermute | solution.py:407
  56.4 0.4 shared_grads_own.1
  56.8 0.0 copy-start.8
  56.8 0.7 collective-permute-done
  57.5 0.7 add.3
  58.3 15.1 %all-to-all-start.2 = ((f32[8,64,128]{2,1,0:T(8,128)}), f32[8,64,128]{2,1,0:T(8,128)S(1)}, u32[]{:S(2)}, u32[]{:S(2)}) async-start(f32[8,64,128]{2,1,0:T(8,128)} %add.3), calls=%async_computation.2 | async-start | bytes 524288 | tf_op jit(solution)/shard_map/all_to_all | solution.py:410
  73.3 0.0 copy-done.8
  73.3 4.0 %finish.1 = (bf16[512,256]{1,0:T(8,128)(2,1)}, bf16[512,256]{1,0:T(8,128)(2,1)}, f32[4,512]{1,0:T(4,128)}, f32[4,512]{1,0:T(4,128)}) custom-call(s32[4]{0:T(128)S(1)} %copy-done.6, f32[4,512]{1,0:T(4,128)S(1)} %copy-done.4, f32[4,512]{1,0:T(4,128)S(1)} %copy-done.5, bf16[512,128]{1,0:T(8,128)(2,1)S(1)} %copy-done.2, bf16[512,128]{1,0:T(8,128)(2,1)S(1)} %copy-done.3, ...), custom_call_target="tpu_custom_call" | custom-call | flops 4000000000 | bytes 20000000 | tf_op jit(solution)/shard_map/finish/pallas_call | solution.py:363
  77.4 7.1 %all-to-all-done.2 = f32[8,64,128]{2,1,0:T(8,128)S(1)} async-done(((f32[8,64,128]{2,1,0:T(8,128)}), f32[8,64,128]{2,1,0:T(8,128)S(1)}, u32[]{:S(2)}, u32[]{:S(2)}) %all-to-all-start.2) | async-done | bytes 262176 | tf_op jit(solution)/shard_map/all_to_all | solution.py:410
  84.4 0.6 fusion
  (1 shorter events, 0.0 us)
Async XLA Ops:
  0.6 17.2 %copy-start.2 = (bf16[512,128]{1,0:T(8,128)(2,1)S(1)}, bf16[512,128]{1,0:T(8,128)(2,1)}, u32[]{:S(2)}) copy-start(bf16[512,128]{1,0:T(8,128)(2,1)} %w_ref.1) | copy-start | bytes 393220
  0.6 17.2 %copy-start.3 = (bf16[512,128]{1,0:T(8,128)(2,1)S(1)}, bf16[512,128]{1,0:T(8,128)(2,1)}, u32[]{:S(2)}) copy-start(bf16[512,128]{1,0:T(8,128)(2,1)} %r_ref.1) | copy-start | bytes 393220
  3.6 14.3 %copy-start = (bf16[512,256]{1,0:T(8,128)(2,1)S(1)}, bf16[512,256]{1,0:T(8,128)(2,1)}, u32[]{:S(2)}) copy-start(bf16[512,256]{1,0:T(8,128)(2,1)} %x_ref.1) | copy-start | bytes 786436
  3.6 14.3 %copy-start.1 = (bf16[512,256]{1,0:T(8,128)(2,1)S(1)}, bf16[512,256]{1,0:T(8,128)(2,1)}, u32[]{:S(2)}) copy-start(bf16[512,256]{1,0:T(8,128)(2,1)} %g_ref.1) | copy-start | bytes 786436
  3.6 14.3 %copy-start.4 = (f32[4,512]{1,0:T(4,128)S(1)}, f32[4,512]{1,0:T(4,128)}, u32[]{:S(2)}) copy-start(f32[4,512]{1,0:T(4,128)} %ld_ref.1) | copy-start | bytes 24580
  3.6 14.3 %copy-start.5 = (f32[4,512]{1,0:T(4,128)S(1)}, f32[4,512]{1,0:T(4,128)}, u32[]{:S(2)}) copy-start(f32[4,512]{1,0:T(4,128)} %dt_ref.1) | copy-start | bytes 24580
  3.6 14.3 %copy-start.6 = (s32[4]{0:T(128)S(1)}, s32[4]{0:T(128)}, u32[]{:S(2)}) copy-start(s32[4]{0:T(128)} %len_ref.1) | copy-start | bytes 52
  3.6 26.9 %all-to-all-start = ((f32[64,1,1152]{2,1,0:T(1,128)}), f32[64,1,1152]{2,1,0:T(1,128)S(1)}, u32[]{:S(2)}, u32[]{:S(2)}) async-start(f32[64,1,1152]{2,1,0:T(1,128)} %bitcast.9), calls=%async_computation | async-start | bytes 589824 | tf_op jit(solution)/shard_map/all_to_all | solution.py:394
  22.3 0.8 copy-start.7
  48.0 9.5 %collective-permute-start = (f32[8,64,128]{2,1,0:T(8,128)S(1)}, f32[8,64,128]{2,1,0:T(8,128)S(1)}, u32[]{:S(2)}, u32[]{:S(2)}) collective-permute-start(f32[8,64,128]{2,1,0:T(8,128)S(1)} %shared_grads_other.1), channel_id=1, source_target_pairs={{0,1},{1,0},{2,3},{3,2},{4,5},{5,4},{6,7},{7,6},{8,9},{9,8},{10,11... | collective-permute-start | bytes 786440 | tf_op jit(solution)/shard_map/ppermute | solution.py:407
  56.8 16.6 %copy-start.8 = (f32[512,256]{1,0:T(8,128)S(1)}, f32[512,256]{1,0:T(8,128)}, u32[]{:S(2)}) copy-start(f32[512,256]{1,0:T(8,128)} %copy-done.7) | copy-start | bytes 1572868
  58.3 26.1 %all-to-all-start.2 = ((f32[8,64,128]{2,1,0:T(8,128)}), f32[8,64,128]{2,1,0:T(8,128)S(1)}, u32[]{:S(2)}, u32[]{:S(2)}) async-start(f32[8,64,128]{2,1,0:T(8,128)} %add.3), calls=%async_computation.2 | async-start | bytes 524288 | tf_op jit(solution)/shard_map/all_to_all | solution.py:410
